TPU v7x, 256 devices: a whole 4x4x8 slice. The times are simulated.
256 devices in a mesh: row: 16 (over z_lo, x), col: 16 (over z_hi, y, core).
Axes of the slice: x: 4, y: 4, z: 8 (z_hi: 2, z_lo: 4; z = z_hi * 4 + z_lo), core: 2. Of those that a mesh axis runs over, the one named last changes fastest.
Arguments:
- token_ids: int32 [16, 16, 128], P('row'), may hold values from 0 to 31999
- embedding: bfloat16 [32000, 1024], P(None, 'col'), may hold values from -6 to 6
- up_one: bfloat16 [16, 1024, 4096], P('row', None, 'col'), may hold values from -0.1875 to 0.1875
- down_one: bfloat16 [16, 4096, 1024], P('row', 'col'), may hold values from -0.09375 to 0.09375
- up_two: bfloat16 [16, 1024, 4096], P('col', None, 'row'), may hold values from -0.1875 to 0.1875
- down_two: bfloat16 [16, 4096, 1024], P('col', 'row'), may hold values from -0.09375 to 0.09375
- moment_up_one: bfloat16 [16, 1024, 4096], P('row', None, 'col'), may hold values from -6 to 6
- moment_down_one: bfloat16 [16, 4096, 1024], P('row', 'col'), may hold values from -6 to 6
- moment_up_two: bfloat16 [16, 1024, 4096], P('col', None, 'row'), may hold values from -6 to 6
- moment_down_two: bfloat16 [16, 4096, 1024], P('col', 'row'), may hold values from -6 to 6
- cotangent: bfloat16 [16, 16, 128, 1024], P('row', 'col'), may hold values from -6 to 6
Outputs:
- new_up_one: bfloat16 [16, 1024, 4096], P('row', None, 'col')
- new_down_one: bfloat16 [16, 4096, 1024], P('row', 'col')
- new_up_two: bfloat16 [16, 1024, 4096], P('col', None, 'row')
- new_down_two: bfloat16 [16, 4096, 1024], P('col', 'row')
- new_moment_up_one: bfloat16 [16, 1024, 4096], P('row', None, 'col')
- new_moment_down_one: bfloat16 [16, 4096, 1024], P('row', 'col')
- new_moment_up_two: bfloat16 [16, 1024, 4096], P('col', None, 'row')
- new_moment_down_two: bfloat16 [16, 4096, 1024], P('col', 'row')
All inputs are finite; a program needn't handle non-finite values.
Results may differ from a plain program's by a relative error of at most 0.019.
Values may be sent and summed in bfloat16 or wider, within the bound.
A program may use at most 128 MiB of HBM per device.

v0:
```python
import jax
import jax.numpy as jnp
from jax import lax
from jax.sharding import PartitionSpec as P

epsilon = 1e-06
momentum_decay = 0.9
outer_rate = 0.7
inner_rate = 0.01


def normalize(values):
    factor = lax.rsqrt(jnp.mean(values * values, axis=-1, keepdims=True) + epsilon)
    return values * factor


def normalize_back(values, upstream):
    factor = lax.rsqrt(jnp.mean(values * values, axis=-1, keepdims=True) + epsilon)
    return factor * upstream - values * (factor * factor * factor) * jnp.mean(
        upstream * values, axis=-1, keepdims=True
    )


def activation(values):
    return jax.nn.gelu(values, approximate=True)


def activation_slope(values, upstream):
    return jax.vjp(activation, values)[1](upstream)[0]


def contract_rows(first_operand, second_operand):
    return lax.dot_general(
        first_operand, second_operand, (((0,), (0,)), ((), ())), preferred_element_type=jnp.float32
    )


def contract_cols(first_operand, second_operand):
    return lax.dot_general(
        first_operand, second_operand, (((1,), (1,)), ((), ())), preferred_element_type=jnp.float32
    )


def outer_update(parameter, moment, gradient, sharers):
    average = gradient / sharers
    new_moment = momentum_decay * moment.astype(jnp.float32) + average
    new_parameter = parameter.astype(jnp.float32) - outer_rate * inner_rate * (
        average + momentum_decay * new_moment
    )
    return (new_parameter.astype(jnp.bfloat16)[None], new_moment.astype(jnp.bfloat16)[None])


def on_device(
    token_ids,
    embedding,
    up_one,
    down_one,
    up_two,
    down_two,
    moment_up_one,
    moment_down_one,
    moment_up_two,
    moment_down_two,
    cotangent,
):
    col_sharers = lax.axis_size("col")
    row_sharers = lax.axis_size("row")
    col_place = lax.axis_index("col")
    tokens = cotangent.shape[2]
    own_cot = cotangent[0, 0]
    ids_flat = token_ids[0].reshape(-1)
    pieces = jnp.take(embedding, ids_flat, axis=0)
    inputs = lax.all_gather(pieces, "col", axis=1, tiled=True)
    normed_one = normalize(inputs.astype(jnp.float32)).astype(jnp.bfloat16)
    pre_one = jnp.dot(normed_one, up_one[0], preferred_element_type=jnp.float32)
    act_one = activation(pre_one).astype(jnp.bfloat16)
    block = act_one
    mixed_one = lax.psum_scatter(
        jnp.dot(block, down_one[0], preferred_element_type=jnp.float32).astype(jnp.bfloat16),
        "col",
        scatter_dimension=0,
        tiled=True,
    ).astype(jnp.float32)
    own_input = lax.dynamic_slice_in_dim(inputs, col_place * tokens, tokens, 0)
    middle = own_input.astype(jnp.float32) + mixed_one
    normed_own = normalize(middle).astype(jnp.bfloat16)
    normed_two, cot_rows = (
        lax.all_gather(normed_own, "row", axis=0, tiled=True),
        lax.all_gather(own_cot, "row", axis=0, tiled=True),
    )
    pre_two = jnp.dot(normed_two, up_two[0], preferred_element_type=jnp.float32)
    act_two = activation(pre_two).astype(jnp.bfloat16)
    grad_down_two = contract_rows(act_two, cot_rows)
    back_two = contract_cols(cot_rows, down_two[0])
    slope_two = activation_slope(pre_two, back_two).astype(jnp.bfloat16)
    grad_up_two = contract_rows(normed_two, slope_two)
    block = slope_two
    back_normed = lax.psum_scatter(
        contract_cols(block, up_two[0]).astype(jnp.bfloat16), "row", scatter_dimension=0, tiled=True
    ).astype(jnp.float32)
    back_middle = (own_cot.astype(jnp.float32) + normalize_back(middle, back_normed)).astype(
        jnp.bfloat16
    )
    cot_group = lax.all_gather(back_middle, "col", axis=0, tiled=True)
    grad_down_one = contract_rows(act_one, cot_group)
    back_one = contract_cols(cot_group, down_one[0])
    slope_one = activation_slope(pre_one, back_one).astype(jnp.bfloat16)
    grad_up_one = contract_rows(normed_one, slope_one)
    new_up_one, new_moment_up_one = outer_update(
        up_one[0], moment_up_one[0], grad_up_one, col_sharers
    )
    new_down_one, new_moment_down_one = outer_update(
        down_one[0], moment_down_one[0], grad_down_one, col_sharers
    )
    new_up_two, new_moment_up_two = outer_update(
        up_two[0], moment_up_two[0], grad_up_two, row_sharers
    )
    new_down_two, new_moment_down_two = outer_update(
        down_two[0], moment_down_two[0], grad_down_two, row_sharers
    )
    return (
        new_up_one,
        new_down_one,
        new_up_two,
        new_down_two,
        new_moment_up_one,
        new_moment_down_one,
        new_moment_up_two,
        new_moment_down_two,
    )


def solution(mesh):
    in_specs = (
        P("row", None, None),
        P(None, "col"),
        P("row", None, "col"),
        P("row", "col", None),
        P("col", None, "row"),
        P("col", "row", None),
        P("row", None, "col"),
        P("row", "col", None),
        P("col", None, "row"),
        P("col", "row", None),
        P("row", "col", None, None),
    )
    out_specs = (
        P("row", None, "col"),
        P("row", "col", None),
        P("col", None, "row"),
        P("col", "row", None),
        P("row", None, "col"),
        P("row", "col", None),
        P("col", None, "row"),
        P("col", "row", None),
    )
    return jax.shard_map(
        on_device, mesh=mesh, in_specs=in_specs, out_specs=out_specs, check_vma=False
    )
```

profile of v0, /device:TPU:1, one launch (start us, length us, event | category | flops | bytes accessed | tf_op | source)
XLA Modules:
  0.0 594.7 jit_solution(13663081932477852762)
XLA Ops:
  7.2 0.0 all-gather.6.cloned.1.call-start
  7.2 0.7 compare_and_fusion
  7.9 0.7 compare_select_fusion
  8.6 8.3 %copy.20 = bf16[32000,64]{1,0:T(8,128)(2,1)} copy(bf16[32000,64]{0,1:T(8,128)(2,1)} %param.12) | data formatting | bytes 8192000 | tf_op args[1]
  17.0 10.0 %gather_fusion = bf16[2048,64]{1,0:T(8,128)(2,1)S(1)} fusion(bf16[32000,64]{1,0:T(8,128)(2,1)} %copy.20, s32[2048]{0:T(1024)S(1)} %broadcast_clamp_fusion), kind=kCustom, calls=%fused_computation | custom fusion | bytes 532480 | tf_op jit(solution)/shard_map/jit(_take)/gather | solution.py:72
  27.0 0.3 broadcast_select_fusion
  27.3 0.0 copy-start.9
  27.3 0.9 copy.21
  28.2 0.0 all-gather.6.cloned.1.call-update
  28.2 0.0 reduce-scatter.3.cloned.1.call-start
  28.3 81.6 %all-gather.6.cloned.1.call-done = bf16[2048,1024]{0,1:T(8,128)(2,1)} async-done(((bf16[2048,64]{0,1:T(8,128)(2,1)}), bf16[2048,1024]{0,1:T(8,128)(2,1)}) %all-gather.6.cloned.1.call-update) | async-done | bytes 4194320 | tf_op jit(solution)/shard_map/all_gather | solution.py:73
  109.9 3.2 fusion
  113.2 0.2 copy-done
  113.4 1.5 fusion.8
  114.9 1.3 copy-done.15
  116.2 3.5 convolution_convert_fusion.1
  119.7 0.0 reduce-scatter.3.cloned.1.call-update
  119.7 0.0 copy-start.3
  119.7 0.0 all-gather.8.cloned.1.call-start
  119.7 1.0 constant_dynamic-slice_fusion
  120.8 0.1 copy.23
  120.9 96.9 %reduce-scatter.3.cloned.1.call-done = bf16[128,1024]{1,0:T(8,128)(2,1)} async-done(((bf16[2048,1024]{1,0:T(8,128)(2,1)}), bf16[128,1024]{1,0:T(8,128)(2,1)}) %reduce-scatter.3.cloned.1.call-update) | async-done | bytes 262160 | tf_op jit(solution)/shard_map/reduce_scatter | solution.py:78
  217.8 1.1 multiply_reduce_fusion
  219.0 1.8 multiply_convert_fusion.3
  220.7 0.0 all-gather.8.cloned.1.call-update
  220.7 0.0 all-gather.12.cloned.1.call-start
  220.8 0.5 all-gather.12.cloned.1.call-update
  221.3 0.0 copy-start.6
  221.3 0.0 reduce-scatter.5.cloned.1.call-start
  221.4 75.8 %all-gather.8.cloned.1.call-done = bf16[2048,1024]{1,0:T(8,128)(2,1)} async-done(((bf16[128,1024]{1,0:T(8,128)(2,1)}), bf16[2048,1024]{1,0:T(8,128)(2,1)}) %all-gather.8.cloned.1.call-update) | async-done | bytes 4194320 | tf_op jit(solution)/shard_map/all_gather | solution.py:88
  297.2 4.8 fusion.60
  301.9 83.5 %all-gather.12.cloned.1.call-done = bf16[1,1,2048,1024]{3,2,1,0:T(8,128)(2,1)} async-done(((bf16[1,1,128,1024]{3,2,1,0:T(8,128)(2,1)}), bf16[1,1,2048,1024]{3,2,1,0:T(8,128)(2,1)}) %all-gather.12.cloned.1.call-update) | async-done | bytes 4194320 | tf_op jit(solution)/shard_map/all_gather | solution.py:89
  385.4 5.2 fusion.23
  390.6 3.2 convolution_convert_fusion
  393.8 0.0 reduce-scatter.5.cloned.1.call-update
  393.9 0.0 copy-start.5
  393.9 0.2 all-gather.10.cloned.1.call-start
  394.1 91.0 %reduce-scatter.5.cloned.1.call-done = bf16[128,1024]{1,0:T(8,128)(2,1)} async-done(((bf16[2048,1024]{1,0:T(8,128)(2,1)}), bf16[128,1024]{1,0:T(8,128)(2,1)}) %reduce-scatter.5.cloned.1.call-update) | async-done | bytes 262160 | tf_op jit(solution)/shard_map/reduce_scatter | solution.py:98
  485.1 1.1 fusion.50
  486.3 1.9 fusion.49
  488.2 0.0 all-gather.10.cloned.1.call-update
  488.2 0.0 copy-start.7
  488.2 4.8 fusion.55
  493.0 0.0 copy-start.8
  493.0 2.6 fusion.57
  495.7 76.7 %all-gather.10.cloned.1.call-done = bf16[2048,1024]{1,0:T(8,128)(2,1)} async-done(((bf16[128,1024]{1,0:T(8,128)(2,1)}), bf16[2048,1024]{1,0:T(8,128)(2,1)}) %all-gather.10.cloned.1.call-update) | async-done | bytes 4194320 | tf_op jit(solution)/shard_map/all_gather | solution.py:104
  572.4 10.1 %fusion.51 = (bf16[1,1024,256]{2,1,0:T(8,128)(2,1)}, bf16[1,1024,256]{2,1,0:T(8,128)(2,1)}) fusion(bf16[1,1024,256]{2,1,0:T(8,128)(2,1)S(1)} %copy-done.8, bf16[1,1024,256]{2,1,0:T(8,128)(2,1)S(1)} %copy-done.10, f32[2048,256]{1,0:T(8,128)} %copy-done.15, bf16[2048,1024]{1,0:T(8,128)(2,1)} %all-gather.10.cloned.1.call-done, ...), kind=kOutput, calls=%fused_computation.65 | convolution fusion | flops 2167144448 | bytes 13115392 | tf_op jit(solution)/shard_map/dot_general | solution.py:33
  582.5 5.4 fusion.53
  (28 shorter events, 0.1 us)
Async XLA Ops:
  7.2 102.8 %all-gather.6.cloned.1.call-start = ((), (), s32[]{:S(2)}) async-start(), calls=%async_computation.2 | async-start | bytes 4456448 | tf_op jit(solution)/shard_map/all_gather | solution.py:73
  27.3 85.8 %copy-start.9 = (bf16[1,1024,256]{2,1,0:T(8,128)(2,1)S(1)}, bf16[1,1024,256]{2,1,0:T(8,128)(2,1)}, u32[]{:S(2)}) copy-start(bf16[1,1024,256]{2,1,0:T(8,128)(2,1)} %param.13) | copy-start | bytes 1572868
  28.2 189.6 %reduce-scatter.3.cloned.1.call-start = ((), (), s32[]{:S(2)}) async-start(), calls=%async_computation.3 | async-start | bytes 4456448 | tf_op jit(solution)/shard_map/reduce_scatter | solution.py:78
  109.9 3.4 copy-start
  113.4 2.8 copy-start.11
  114.8 1.3 copy-start.15
  119.7 177.5 %copy-start.3 = (bf16[1,1024,256]{2,1,0:T(8,128)(2,1)S(1)}, bf16[1,1024,256]{2,1,0:T(8,128)(2,1)}, u32[]{:S(2)}) copy-start(bf16[1,1024,256]{2,1,0:T(8,128)(2,1)} %param.15) | copy-start | bytes 1572868
  119.7 177.5 %all-gather.8.cloned.1.call-start = ((), (), s32[]{:S(2)}) async-start(), calls=%async_computation.4 | async-start | bytes 4456448 | tf_op jit(solution)/shard_map/all_gather | solution.py:88
  220.7 164.7 %all-gather.12.cloned.1.call-start = ((), (), s32[]{:S(2)}) async-start(), calls=%async_computation.7 | async-start | bytes 4456448 | tf_op jit(solution)/shard_map/all_gather | solution.py:89
  221.3 164.1 %copy-start.6 = (bf16[1,256,1024]{2,1,0:T(8,128)(2,1)S(1)}, bf16[1,256,1024]{2,1,0:T(8,128)(2,1)}, u32[]{:S(2)}) copy-start(bf16[1,256,1024]{2,1,0:T(8,128)(2,1)} %param.16) | copy-start | bytes 1572868
  221.3 263.8 %reduce-scatter.5.cloned.1.call-start = ((), (), s32[]{:S(2)}) async-start(), calls=%async_computation.5 | async-start | bytes 4456448 | tf_op jit(solution)/shard_map/reduce_scatter | solution.py:98
  393.8 91.3 %copy-start.1 = (bf16[128,1024]{1,0:T(8,128)(2,1)S(1)}, bf16[128,1024]{1,0:T(8,128)(2,1)}, u32[]{:S(2)}) copy-start(bf16[128,1024]{1,0:T(8,128)(2,1)} %reduce-scatter.3.cloned.1.call-done) | copy-start | bytes 786436
  393.8 92.4 %copy-start.2 = (bf16[1,1,128,1024]{3,2,1,0:T(8,128)(2,1)S(1)}, bf16[1,1,128,1024]{3,2,1,0:T(8,128)(2,1)}, u32[]{:S(2)}) copy-start(bf16[1,1,128,1024]{3,2,1,0:T(8,128)(2,1)} %param.21) | copy-start | bytes 786436
  393.9 94.3 %copy-start.5 = (bf16[1,1024,256]{2,1,0:T(8,128)(2,1)S(1)}, bf16[1,1024,256]{2,1,0:T(8,128)(2,1)}, u32[]{:S(2)}) copy-start(bf16[1,1024,256]{2,1,0:T(8,128)(2,1)} %param.19) | copy-start | bytes 1572868
  393.9 178.5 %all-gather.10.cloned.1.call-start = ((), (), s32[]{:S(2)}) async-start(), calls=%async_computation.6 | async-start | bytes 4456448 | tf_op jit(solution)/shard_map/all_gather | solution.py:104
  488.2 4.8 copy-start.4
  488.2 4.8 copy-start.7
  488.2 4.8 copy-start.14
  493.0 79.4 %copy-start.8 = (bf16[1,1024,256]{2,1,0:T(8,128)(2,1)S(1)}, bf16[1,1024,256]{2,1,0:T(8,128)(2,1)}, u32[]{:S(2)}) copy-start(bf16[1,1024,256]{2,1,0:T(8,128)(2,1)} %param.17) | copy-start | bytes 1572868
  493.0 79.4 %copy-start.10 = (bf16[1,1024,256]{2,1,0:T(8,128)(2,1)S(1)}, bf16[1,1024,256]{2,1,0:T(8,128)(2,1)}, u32[]{:S(2)}) copy-start(bf16[1,1024,256]{2,1,0:T(8,128)(2,1)} %param.13) | copy-start | bytes 1572868
  493.0 79.4 %copy-start.12 = (bf16[1,256,1024]{2,1,0:T(8,128)(2,1)S(1)}, bf16[1,256,1024]{2,1,0:T(8,128)(2,1)}, u32[]{:S(2)}) copy-start(bf16[1,256,1024]{2,1,0:T(8,128)(2,1)} %param.14) | copy-start | bytes 1572868
  495.7 86.8 %copy-start.13 = (bf16[1,256,1024]{2,1,0:T(8,128)(2,1)S(1)}, bf16[1,256,1024]{2,1,0:T(8,128)(2,1)}, u32[]{:S(2)}) copy-start(bf16[1,256,1024]{2,1,0:T(8,128)(2,1)} %param.18) | copy-start | bytes 1572868
Sparse Core Ops, SparseCore 0:
  28.4 81.5 all-gather.5
  119.8 97.9 reduce-scatter.2
  220.9 76.2 all-gather.7
  299.0 86.4 all-gather.11
  394.0 91.0 reduce-scatter.4
  488.7 83.6 all-gather.9
where the time goes:
time: 595 us
  waiting for transfers between devices  506 us (85%)
  matrix products  40.9 us (7%)
  local copies, waits for them, and re-layouts  22 us (4%)
  between operations  14.3 us (2%)
  other arithmetic  10.9 us (2%)
    reduce_scatter x1, waiting for transfers between devices, on_device(): lax.psum_scatter(jnp.dot(block, down_one[0], preferred_element_type=jnp.f...  96.9 us
    reduce_scatter x1, waiting for transfers between devices, on_device(): lax.psum_scatter(contract_cols(block, up_two[0]).astype(jnp.bfloat16), 'r...  91 us
    all_gather x1, waiting for transfers between devices, on_device(): lax.all_gather(own_cot, 'row', axis=0, tiled=True)  83.5 us
    all_gather x1, waiting for transfers between devices, on_device(): inputs = lax.all_gather(pieces, 'col', axis=1, tiled=True)  81.6 us
    all_gather x1, waiting for transfers between devices, on_device(): cot_group = lax.all_gather(back_middle, 'col', axis=0, tiled=True)  76.7 us
    all_gather x1, waiting for transfers between devices, on_device(): lax.all_gather(normed_own, 'row', axis=0, tiled=True)  75.8 us
    dot_general x4, matrix products, contract_rows(): lax.dot_general(first_operand, second_operand, (((0,), (0,)), ((), ())),...  22.8 us
  transfers between devices with their start and end apart: 6, of which 6 were waited for; matrix products, arithmetic and copies ran while one was open for 2% of the time, Pallas kernels for 0%

commit v1 on v0

v1 whole, which is shorter than its diff:
```python
import functools

import jax
import jax.numpy as jnp
from jax import lax
from jax.experimental import pallas as pl
from jax.experimental.pallas import tpu as pltpu
from jax.sharding import PartitionSpec as P

epsilon = 1e-06
momentum_decay = 0.9
outer_rate = 0.7
inner_rate = 0.01
MESH = pl.DeviceIdType.MESH
RING = 4
TOK = 128


def activation(values):
    return jax.nn.gelu(values, approximate=True)


def activation_slope(values, upstream):
    return jax.vjp(activation, values)[1](upstream)[0]


def contract_rows(first_operand, second_operand):
    return lax.dot_general(
        first_operand, second_operand, (((0,), (0,)), ((), ())), preferred_element_type=jnp.float32
    )


def contract_cols(first_operand, second_operand):
    return lax.dot_general(
        first_operand, second_operand, (((1,), (1,)), ((), ())), preferred_element_type=jnp.float32
    )


def outer_update(parameter, moment, gradient, sharers):
    average = gradient / sharers
    new_moment = momentum_decay * moment.astype(jnp.float32) + average
    new_parameter = parameter.astype(jnp.float32) - outer_rate * inner_rate * (
        average + momentum_decay * new_moment
    )
    return (new_parameter.astype(jnp.bfloat16)[None], new_moment.astype(jnp.bfloat16)[None])


class Place:
    def __init__(self):
        row, col = lax.axis_index("row"), lax.axis_index("col")
        self.zl, self.x = row // 4, row % 4
        self.zh, self.y, self.k = col // 8, (col // 2) % 4, col % 2
        self.stay = (self.zl // 2) == self.k
        other_zl = (self.zl + 2) % 4
        self.swap = (other_zl * 4 + self.x, self.zh * 8 + self.y * 2 + (1 - self.k))


class ColGroup:
    def __init__(self, place):
        self.place = place
        self.p, self.t, self.k = place.zh, place.y, place.k

    def device(self, p, t, k):
        return (self.place.zl * 4 + self.place.x, p * 8 + t * 2 + k)

    @staticmethod
    def slot(p, t, k):
        return p * 8 + t * 2 + k


class RowGroup:
    def __init__(self, place):
        self.place = place
        self.p, self.t, self.k = place.zl % 2, place.x, place.k
        self.half = place.zl // 2

    def device(self, p, t, k):
        return ((self.half * 2 + p) * 4 + t, self.place.zh * 8 + self.place.y * 2 + k)

    @staticmethod
    def slot(p, t, k):
        return (2 * k + p) * 4 + t


def near(group):
    p, t, k = group.p, group.t, group.k
    up, down = (t + 1) % RING, (t + RING - 1) % RING
    return {
        "pair": group.device(1 - p, t, k),
        "sibling": group.device(p, t, 1 - k),
        "up": group.device(p, up, k),
        "down": group.device(p, down, k),
    }


def greet(devices):
    barrier = pltpu.get_barrier_semaphore()
    for device in devices:
        pl.semaphore_signal(barrier, inc=1, device_id=device, device_id_type=MESH)
    pl.semaphore_wait(barrier, len(devices))


class Mail:
    def __init__(self, send_sem, recv_sem):
        self.send_sem, self.recv_sem = send_sem, recv_sem
        self.sent = []

    def copy(self, number, src, dst, device):
        return pltpu.make_async_remote_copy(
            src_ref=src,
            dst_ref=dst,
            send_sem=self.send_sem.at[number],
            recv_sem=self.recv_sem.at[number],
            device_id=device,
            device_id_type=MESH,
        )

    def send(self, number, src, dst, device):
        copy = self.copy(number, src, dst, device)
        copy.start()
        self.sent.append(copy)

    def arrived(self, number, ref, device):
        self.copy(number, ref, ref, device).wait_recv()

    def finish(self):
        for copy in self.sent:
            copy.wait_send()
        self.sent = []


GATHER_MESSAGES = 17


class Gather:
    def __init__(self, group, mail, base, region, half):
        self.g, self.mail, self.base, self.region, self.half = group, mail, base, region, half
        self.peers = near(group)

    def send(self, m, ref, to):
        self.mail.send(self.base + m, ref, ref, self.peers[to])

    def got(self, m, ref):
        self.mail.arrived(self.base + m, ref, self.peers["sibling"])

    def start(self):
        g = self.g
        own = self.region(g.p, g.t, g.k)
        self.send(0, own, "pair")
        self.send(2, own, "up")
        self.send(3, own, "down")
        self.send(1, own, "sibling")

    def pair_arrived(self):
        g = self.g
        q = 1 - g.p
        ref = self.region(q, g.t, g.k)
        self.got(0, ref)
        self.send(4, ref, "up")
        self.send(5, ref, "down")
        self.send(6, ref, "sibling")

    def ring_arrived(self, which):
        g = self.g
        q, first, fwd = ((g.p, 2, 7), (1 - g.p, 4, 11))[which]
        before, after = (g.t + RING - 1) % RING, (g.t + 1) % RING
        ref = self.region(q, before, g.k)
        self.got(first, ref)
        self.send(fwd, self.half(q, before, g.k, 0), "up")
        self.send(fwd + 1, ref, "sibling")
        ref = self.region(q, after, g.k)
        self.got(first + 1, ref)
        self.send(fwd + 2, self.half(q, after, g.k, 1), "down")
        self.send(fwd + 3, ref, "sibling")

    def far_arrived(self, which):
        g = self.g
        q, fwd, last = ((g.p, 7, 15), (1 - g.p, 11, 16))[which]
        far = (g.t + 2) % RING
        self.got(fwd, self.half(q, far, g.k, 0))
        self.got(fwd + 2, self.half(q, far, g.k, 1))
        self.send(last, self.region(q, far, g.k), "sibling")

    def sibling_arrived(self):
        g = self.g
        before, after, far = (g.t + RING - 1) % RING, (g.t + 1) % RING, (g.t + 2) % RING
        o = 1 - g.k
        for m, q, t in (
            (1, g.p, g.t),
            (6, 1 - g.p, g.t),
            (8, g.p, before),
            (10, g.p, after),
            (12, 1 - g.p, before),
            (14, 1 - g.p, after),
            (15, g.p, far),
            (16, 1 - g.p, far),
        ):
            self.got(m, self.region(q, t, o))

    def run(self):
        self.start()
        self.pair_arrived()
        self.ring_arrived(0)
        self.ring_arrived(1)
        self.far_arrived(0)
        self.far_arrived(1)
        self.sibling_arrived()


SCATTER_MESSAGES = 8 + 4 + 8 + 1


def scatter_sum(group, mail, base, part, from_sibling, sums, from_far, from_near, from_pair):
    f32, b16 = jnp.float32, jnp.bfloat16
    p, t, k = group.p, group.t, group.k
    peers = near(group)
    up, down, far = (t + 1) % RING, (t + RING - 1) % RING, (t + 2) % RING
    top, low = pl.ds(0, TOK // 2), pl.ds(TOK // 2, TOK // 2)
    order = [(q, s) for q in (1, 0) for s in (2, 1, 3, 0)]

    def place(q, s):
        return (1 - p if q else p), (t + s) % RING

    def cell(q, s):
        return q * 4 + s

    for q, s in order:
        side, at = place(q, s)
        mail.send(
            base + cell(q, s),
            part.at[group.slot(side, at, 1 - k)],
            from_sibling.at[cell(q, s)],
            peers["sibling"],
        )

    def pair_sum(q, s):
        side, at = place(q, s)
        mail.arrived(base + cell(q, s), from_sibling.at[cell(q, s)], peers["sibling"])
        sums[cell(q, s)] = (
            part[group.slot(side, at, k)].astype(f32) + from_sibling[cell(q, s)].astype(f32)
        ).astype(b16)

    far_base, near_base, pair_base = base + 8, base + 12, base + 20
    for q in (1, 0):
        pair_sum(q, 2)
        mail.send(far_base + 2 * q, sums.at[cell(q, 2), top], from_far.at[2 * q], peers["up"])
        mail.send(far_base + 2 * q + 1, sums.at[cell(q, 2), low], from_far.at[2 * q + 1], peers["down"])
        pair_sum(q, 1)
        mail.send(near_base + 4 * q, sums.at[cell(q, 1), low], from_near.at[2 * q, low], peers["up"])
        pair_sum(q, 3)
        mail.send(near_base + 4 * q + 1, sums.at[cell(q, 3), top], from_near.at[2 * q + 1, top], peers["down"])
        pair_sum(q, 0)
    for q in (1, 0):
        mail.arrived(far_base + 2 * q, from_far.at[2 * q], peers["sibling"])
        sums[cell(q, 1), top] = (
            sums[cell(q, 1), top].astype(f32) + from_far[2 * q].astype(f32)
        ).astype(b16)
        mail.send(near_base + 4 * q + 2, sums.at[cell(q, 1), top], from_near.at[2 * q, top], peers["up"])
        mail.arrived(far_base + 2 * q + 1, from_far.at[2 * q + 1], peers["sibling"])
        sums[cell(q, 3), low] = (
            sums[cell(q, 3), low].astype(f32) + from_far[2 * q + 1].astype(f32)
        ).astype(b16)
        mail.send(near_base + 4 * q + 3, sums.at[cell(q, 3), low], from_near.at[2 * q + 1, low], peers["down"])

    def total(q):
        mail.arrived(near_base + 4 * q, from_near.at[2 * q, low], peers["sibling"])
        mail.arrived(near_base + 4 * q + 1, from_near.at[2 * q + 1, top], peers["sibling"])
        mail.arrived(near_base + 4 * q + 2, from_near.at[2 * q, top], peers["sibling"])
        mail.arrived(near_base + 4 * q + 3, from_near.at[2 * q + 1, low], peers["sibling"])
        return (
            sums[cell(q, 0)].astype(f32)
            + from_near[2 * q].astype(f32)
            + from_near[2 * q + 1].astype(f32)
        )

    sums[cell(1, 0)] = total(1).astype(b16)
    mail.send(pair_base, sums.at[cell(1, 0)], from_pair, peers["pair"])
    mine = total(0)
    mail.arrived(pair_base, from_pair, peers["sibling"])
    return mine + from_pair[...].astype(f32)


def scatter_scratch(width):
    b16 = jnp.bfloat16
    return [
        pltpu.VMEM((8, TOK, width), b16),
        pltpu.VMEM((8, TOK, width), b16),
        pltpu.VMEM((4, TOK // 2, width), b16),
        pltpu.VMEM((4, TOK, width), b16),
        pltpu.VMEM((TOK, width), b16),
    ]


def token_regions(buf, slot):
    def region(p, t, k):
        return buf.at[slot(p, t, k)]

    def half(p, t, k, h):
        return buf.at[slot(p, t, k), pl.ds(h * (TOK // 2), TOK // 2)]

    return region, half


def swap_or_keep(place, mail, number, src, dst):
    @pl.when(place.stay)
    def _():
        dst[...] = src[...]

    @pl.when(jnp.logical_not(place.stay))
    def _():
        mail.copy(number, src, dst, place.swap).start()


def swap_wait(place, mail, number, src, dst):
    @pl.when(jnp.logical_not(place.stay))
    def _():
        mail.copy(number, src, dst, place.swap).wait()


def first_kernel(
    pieces, cot, up_two, down_two, inputs, cots, up_out, down_out, wide, other, send_sem, recv_sem
):
    place = Place()
    col, row = ColGroup(place), RowGroup(place)
    mail = Mail(send_sem, recv_sem)
    peers_c, peers_r = near(col), near(row)
    greet(
        [peers_c["sibling"], peers_c["pair"], peers_c["up"], peers_c["down"]]
        + [peers_r["pair"], peers_r["up"], peers_r["down"], place.swap]
    )
    k = place.k
    rows = pieces.shape[0] // 2
    own = pieces[...]
    wide[...] = jnp.concatenate([own, own], axis=1)
    mail.send(0, wide.at[pl.ds((1 - k) * rows, rows)], other, peers_c["sibling"])
    slot = row.slot(row.p, row.t, row.k)
    swap_slot = row.slot(row.p, row.t, 1 - row.k)

    @pl.when(place.stay)
    def _():
        cots[slot] = cot[...]

    @pl.when(jnp.logical_not(place.stay))
    def _():
        mail.copy(1, cot, cots.at[swap_slot], place.swap).start()

    mail.arrived(0, other, peers_c["sibling"])
    lane = lax.broadcasted_iota(jnp.int32, (rows, 128), 1) // 64
    here = pl.ds(pl.multiple_of((place.zh * 4 + place.y) * 128, 128), 128)
    inputs[pl.ds(k * rows, rows), here] = jnp.where(
        lane == k, wide[pl.ds(k * rows, rows)], other[...]
    )

    def region(p, t, k):
        return inputs.at[pl.ds(k * rows, rows), pl.ds(pl.multiple_of((p * 4 + t) * 128, 128), 128)]

    def half(p, t, k, h):
        return inputs.at[
            pl.ds(k * rows + h * (rows // 2), rows // 2),
            pl.ds(pl.multiple_of((p * 4 + t) * 128, 128), 128),
        ]

    tokens = Gather(col, mail, 4, region, half)
    tokens.start()
    swap_wait(place, mail, 1, cot, cots.at[swap_slot])
    upstream = Gather(row, mail, 4 + GATHER_MESSAGES, *token_regions(cots, row.slot))
    upstream.start()
    swap_or_keep(place, mail, 2, up_two, up_out)
    swap_or_keep(place, mail, 3, down_two, down_out)
    for gather in (tokens, upstream):
        gather.pair_arrived()
    for which in (0, 1):
        for gather in (tokens, upstream):
            gather.ring_arrived(which)
    for which in (0, 1):
        for gather in (tokens, upstream):
            gather.far_arrived(which)
    for gather in (tokens, upstream):
        gather.sibling_arrived()
    swap_wait(place, mail, 2, up_two, up_out)
    swap_wait(place, mail, 3, down_two, down_out)
    mail.finish()


def second_kernel(part, own_input, middle, normed, mine, *scratch):
    *scatter, send_sem, recv_sem = scratch
    place = Place()
    col, row = ColGroup(place), RowGroup(place)
    mail = Mail(send_sem, recv_sem)
    peers_c, peers_r = near(col), near(row)
    greet(
        [peers_c["sibling"], peers_c["pair"], peers_c["up"], peers_c["down"]]
        + [peers_r["pair"], peers_r["up"], peers_r["down"], place.swap]
    )
    mixed = scatter_sum(col, mail, 1, part, *scatter)
    values = own_input[...].astype(jnp.float32) + mixed
    middle[...] = values
    factor = lax.rsqrt(jnp.mean(values * values, axis=-1, keepdims=True) + epsilon)
    mine[...] = (values * factor).astype(jnp.bfloat16)
    slot = row.slot(row.p, row.t, row.k)
    swap_slot = row.slot(row.p, row.t, 1 - row.k)

    @pl.when(place.stay)
    def _():
        normed[slot] = mine[...]

    @pl.when(jnp.logical_not(place.stay))
    def _():
        mail.copy(0, mine, normed.at[swap_slot], place.swap).start()

    swap_wait(place, mail, 0, mine, normed.at[swap_slot])
    Gather(row, mail, 1 + SCATTER_MESSAGES, *token_regions(normed, row.slot)).run()
    mail.finish()


def third_kernel(
    part, middle, cot, grad_up, grad_down, group, grad_up_out, grad_down_out, mine, back, *scratch
):
    *scatter, send_sem, recv_sem = scratch
    place = Place()
    col, row = ColGroup(place), RowGroup(place)
    mail = Mail(send_sem, recv_sem)
    peers_c, peers_r = near(col), near(row)
    greet(
        [peers_c["sibling"], peers_c["pair"], peers_c["up"], peers_c["down"]]
        + [peers_r["pair"], peers_r["up"], peers_r["down"], place.swap]
    )
    mine[...] = scatter_sum(row, mail, 3, part, *scatter).astype(jnp.bfloat16)
    swap_or_keep(place, mail, 0, mine, back)
    swap_wait(place, mail, 0, mine, back)
    swap_or_keep(place, mail, 1, grad_up, grad_up_out)
    swap_or_keep(place, mail, 2, grad_down, grad_down_out)
    upstream = back[...].astype(jnp.float32)
    values = middle[...]
    factor = lax.rsqrt(jnp.mean(values * values, axis=-1, keepdims=True) + epsilon)
    through = factor * upstream - values * (factor * factor * factor) * jnp.mean(
        upstream * values, axis=-1, keepdims=True
    )
    group[col.slot(col.p, col.t, col.k)] = (cot[...].astype(jnp.float32) + through).astype(
        jnp.bfloat16
    )
    Gather(col, mail, 3 + SCATTER_MESSAGES, *token_regions(group, col.slot)).run()
    swap_wait(place, mail, 1, grad_up, grad_up_out)
    swap_wait(place, mail, 2, grad_down, grad_down_out)
    mail.finish()


def call(kernel, name, out_shape, args, scratch, messages, number):
    vmem = pl.BlockSpec(memory_space=pltpu.VMEM)
    return pl.pallas_call(
        kernel,
        name=name,
        out_shape=out_shape,
        in_specs=[vmem] * len(args),
        out_specs=[vmem] * len(out_shape),
        scratch_shapes=scratch
        + [pltpu.SemaphoreType.DMA((messages,)), pltpu.SemaphoreType.DMA((messages,))],
        compiler_params=pltpu.CompilerParams(
            collective_id=number, has_side_effects=True, vmem_limit_bytes=48 * 2**20
        ),
    )(*args)


def on_device(
    token_ids,
    embedding,
    up_one,
    down_one,
    up_two,
    down_two,
    moment_up_one,
    moment_down_one,
    moment_up_two,
    moment_down_two,
    cotangent,
):
    b16, f32 = jnp.bfloat16, jnp.float32
    sharers = 16
    col_place = lax.axis_index("col")
    width = cotangent.shape[3]
    own_cot = cotangent[0, 0]
    ids_flat = token_ids[0].reshape(-1)
    tokens = ids_flat.shape[0]
    pieces = embedding.at[ids_flat].get(mode="promise_in_bounds")
    whole = jax.ShapeDtypeStruct((16, TOK, width), b16)
    inputs, cots, up_home, down_home = call(
        first_kernel,
        "first",
        [
            jax.ShapeDtypeStruct((tokens, width), b16),
            whole,
            jax.ShapeDtypeStruct(up_two.shape[1:], b16),
            jax.ShapeDtypeStruct(down_two.shape[1:], b16),
        ],
        [pieces, own_cot, up_two[0], down_two[0]],
        [pltpu.VMEM((tokens, 128), b16), pltpu.VMEM((tokens // 2, 128), b16)],
        4 + 2 * GATHER_MESSAGES,
        0,
    )
    wide = inputs.astype(f32)
    factor = lax.rsqrt(jnp.mean(wide * wide, axis=-1, keepdims=True) + epsilon)
    normed_one = (wide * factor).astype(b16)
    pre_one = jnp.dot(normed_one, up_one[0], preferred_element_type=f32)
    act_one = activation(pre_one).astype(b16)
    part_one = jnp.dot(act_one, down_one[0], preferred_element_type=f32).astype(b16)
    own_input = lax.dynamic_slice_in_dim(inputs, col_place * TOK, TOK, 0)
    middle, normed_two = call(
        second_kernel,
        "second",
        [jax.ShapeDtypeStruct((TOK, width), f32), whole],
        [part_one.reshape(16, TOK, width), own_input],
        [pltpu.VMEM((TOK, width), b16)] + scatter_scratch(width),
        1 + SCATTER_MESSAGES + GATHER_MESSAGES,
        1,
    )
    normed_two = normed_two.reshape(tokens, width)
    cot_rows = cots.reshape(tokens, width)
    pre_two = jnp.dot(normed_two, up_home, preferred_element_type=f32)
    act_two = activation(pre_two).astype(b16)
    grad_down_two = contract_rows(act_two, cot_rows).astype(b16)
    back_two = contract_cols(cot_rows, down_home)
    slope_two = activation_slope(pre_two, back_two).astype(b16)
    grad_up_two = contract_rows(normed_two, slope_two).astype(b16)
    part_two = contract_cols(slope_two, up_home).astype(b16)
    group, grad_up_two, grad_down_two = call(
        third_kernel,
        "third",
        [
            whole,
            jax.ShapeDtypeStruct(up_two.shape[1:], b16),
            jax.ShapeDtypeStruct(down_two.shape[1:], b16),
        ],
        [part_two.reshape(16, TOK, width), middle, own_cot, grad_up_two, grad_down_two],
        [pltpu.VMEM((TOK, width), b16)] * 2 + scatter_scratch(width),
        3 + SCATTER_MESSAGES + GATHER_MESSAGES,
        2,
    )
    group = group.reshape(tokens, width)
    grad_down_one = contract_rows(act_one, group)
    back_one = contract_cols(group, down_one[0])
    slope_one = activation_slope(pre_one, back_one).astype(b16)
    grad_up_one = contract_rows(normed_one, slope_one)
    new_up_one, new_moment_up_one = outer_update(up_one[0], moment_up_one[0], grad_up_one, sharers)
    new_down_one, new_moment_down_one = outer_update(
        down_one[0], moment_down_one[0], grad_down_one, sharers
    )
    new_up_two, new_moment_up_two = outer_update(
        up_two[0], moment_up_two[0], grad_up_two.astype(f32), sharers
    )
    new_down_two, new_moment_down_two = outer_update(
        down_two[0], moment_down_two[0], grad_down_two.astype(f32), sharers
    )
    return (
        new_up_one,
        new_down_one,
        new_up_two,
        new_down_two,
        new_moment_up_one,
        new_moment_down_one,
        new_moment_up_two,
        new_moment_down_two,
    )


def solution(mesh):
    in_specs = (
        P("row", None, None),
        P(None, "col"),
        P("row", None, "col"),
        P("row", "col", None),
        P("col", None, "row"),
        P("col", "row", None),
        P("row", None, "col"),
        P("row", "col", None),
        P("col", None, "row"),
        P("col", "row", None),
        P("row", "col", None, None),
    )
    out_specs = (
        P("row", None, "col"),
        P("row", "col", None),
        P("col", None, "row"),
        P("col", "row", None),
        P("row", None, "col"),
        P("row", "col", None),
        P("col", None, "row"),
        P("col", "row", None),
    )
    return jax.shard_map(
        on_device, mesh=mesh, in_specs=in_specs, out_specs=out_specs, check_vma=False
    )
```

time: 595 us -> 252 us (0.42)
  waiting for transfers between devices: 506 us -> 0 us
  Pallas kernels: 0 us -> 198 us
  between operations: 14.3 us -> 0.92 us
  matrix products: 40.9 us -> 30.2 us
  other arithmetic: 10.9 us -> 3.25 us
    all_gather x4 -> x0, waiting for transfers between devices: 318 us -> none  [the longest x1 83.5 us: on_device(): lax.all_gather(own_cot, 'row', axis=0, tiled=True)]
    pallas_call x0 -> x3, Pallas kernels: none -> 198 us  [call(): pl.pallas_call(kernel, name=name, out_shape=out_shape, in_specs=[vmem] *...]
    reduce_scatter x2 -> x0, waiting for transfers between devices: 188 us -> none  [the longest x1 96.9 us: on_device(): lax.psum_scatter(jnp.dot(block, down_one[0], preferred_element_type=jnp.f...]
  transfers between devices with their start and end apart: 6 -> 0, of which waited for: 6 -> 0; matrix products, arithmetic and copies ran while one was open for 2% -> 0% of each run, Pallas kernels for 0% -> 0%
where the time goes in v1:
time: 252 us
  Pallas kernels  198 us (79%)
  matrix products  30.2 us (12%)
  local copies, waits for them, and re-layouts  19.6 us (8%)
  other arithmetic  3.25 us (1%)
    pallas_call x3, Pallas kernels, call(): pl.pallas_call(kernel, name=name, out_shape=out_shape, in_specs=[vmem] *...  198 us
    dot_general x4, matrix products, contract_rows(): lax.dot_general(first_operand, second_operand, (((0,), (0,)), ((), ())),...  18.5 us
    gather x1, local copies, waits for them, and re-layouts, on_device(): pieces = embedding.at[ids_flat].get(mode='promise_in_bounds')  10.1 us
    unnamed x31, local copies, waits for them, and re-layouts  8.57 us

profile of v1, /device:TPU:1, one launch (start us, length us, event | category | flops | bytes accessed | tf_op | source)
XLA Modules:
  0.0 251.6 jit_solution(181937540654395984)
XLA Ops:
  0.6 0.0 copy-start.4
  0.6 8.3 %copy.19 = bf16[32000,64]{1,0:T(8,128)(2,1)} copy(bf16[32000,64]{0,1:T(8,128)(2,1)} %param.12) | data formatting | bytes 8192000 | tf_op args[1]
  8.9 0.0 copy-done.4
  9.0 0.0 copy-start
  9.0 0.0 copy-start.1
  9.0 0.0 copy-start.2
  9.0 10.1 %gather_fusion = bf16[2048,64]{1,0:T(8,128)(2,1)S(1)} fusion(bf16[32000,64]{1,0:T(8,128)(2,1)} %copy.19, s32[2048]{0:T(1024)S(1)} %broadcast_clamp_fusion), kind=kCustom, calls=%fused_computation | custom fusion | bytes 532480 | tf_op jit(solution)/shard_map/gather | solution.py:484
  19.1 0.0 copy-done
  19.1 0.0 copy-done.1
  19.1 0.0 copy-done.2
  19.1 0.0 copy-start.9
  19.1 55.9 %first.1 = (bf16[2048,1024]{1,0:T(8,128)(2,1)}, bf16[16,128,1024]{2,1,0:T(8,128)(2,1)}, bf16[1024,256]{1,0:T(8,128)(2,1)S(1)}, bf16[256,1024]{1,0:T(8,128)(2,1)S(1)}) custom-call(bf16[2048,64]{1,0:T(8,128)(2,1)S(1)} %gather_fusion, bf16[128,1024]{1,0:T(8,128)(2,1)S(1)} %bitcast.95, bf16[1024,256]{1,0:T(8,128)(2,1)S(1)} %bitcast.98, ...), custom_call_target="tpu_custom_call" | custom-call | tf_op jit(solution)/shard_map/first/pallas_call | solution.py:450
  75.0 0.0 copy-start.3
  75.0 3.2 %fusion = f32[2048]{0:T(1024)S(1)} fusion(bf16[2048,1024]{1,0:T(8,128)(2,1)} %get-tuple-element.17), kind=kLoop, calls=%fused_computation.3 | loop fusion | flops 6289408 | bytes 4202496 | tf_op jit(solution)/shard_map/reduce_sum | solution.py:501
  78.3 0.0 copy-done.9
  78.3 0.2 copy-done.3
  78.5 0.0 copy-start.11
  78.5 1.3 fusion.18
  79.8 0.0 copy-done.11
  79.8 0.0 copy-start.13
  79.8 3.4 %convolution_convert_fusion.1 = bf16[2048,1024]{1,0:T(8,128)(2,1)} fusion(bf16[1,256,1024]{2,1,0:T(8,128)(2,1)S(1)} %copy-done.11, f32[2048,256]{1,0:T(8,128)S(1)} %fusion.18), kind=kOutput, calls=%fused_computation.6 | convolution fusion | flops 1080557568 | bytes 6815744 | tf_op jit(solution)/shard_map/dot_general | solution.py:505
  83.3 0.0 copy-done.13
  83.3 1.0 constant_dynamic-slice_fusion.own_input
  84.3 0.0 copy-start.5
  84.3 61.8 %second.1 = (f32[128,1024]{1,0:T(8,128)S(1)}, bf16[16,128,1024]{2,1,0:T(8,128)(2,1)S(1)}) custom-call(bf16[16,128,1024]{2,1,0:T(8,128)(2,1)} %bitcast.102, bf16[128,1024]{1,0:T(8,128)(2,1)S(1)} %constant_dynamic-slice_fusion.own_input), custom_call_target="tpu_custom_call" | custom-call | tf_op jit(solution)/shard_map/second/pallas_call | solution.py:450
  146.1 0.0 copy-done.5
  146.1 1.3 fusion.70
  147.4 2.4 fusion.15
  149.8 1.3 convolution_convert_fusion.3.grad_up
  151.1 3.3 %convolution_convert_fusion = bf16[2048,1024]{1,0:T(8,128)(2,1)} fusion(bf16[2048,256]{1,0:T(8,128)(2,1)S(1)} %get-tuple-element.34, bf16[1024,256]{1,0:T(8,128)(2,1)S(1)} %get-tuple-element.21), kind=kOutput, calls=%fused_computation.5 | convolution fusion | flops 1075838976 | bytes 5767168 | tf_op jit(solution)/shard_map/dot_general | solution.py:34
  154.4 1.5 convolution_convert_fusion.2.grad_down
  155.9 0.0 copy-start.6
  155.9 0.0 copy-start.7
  155.9 0.0 copy-start.12
  155.9 0.0 copy-start.14
  155.9 79.9 %third.1 = (bf16[16,128,1024]{2,1,0:T(8,128)(2,1)}, bf16[1024,256]{1,0:T(8,128)(2,1)S(1)}, bf16[256,1024]{1,0:T(8,128)(2,1)S(1)}) custom-call(bf16[16,128,1024]{2,1,0:T(8,128)(2,1)} %bitcast.101, f32[128,1024]{1,0:T(8,128)S(1)} %get-tuple-element.22.middle, bf16[128,1024]{1,0:T(8,128)(2,1)S(1)} %bitcast.96, ...), custom_call_target="tpu_custom_call" | custom-call | tf_op jit(solution)/shard_map/third/pallas_call | solution.py:450
  235.9 0.0 copy-done.6
  235.9 0.0 copy-done.7
  235.9 0.0 copy-done.12
  235.9 0.0 copy-done.14
  235.9 0.0 copy-start.8
  235.9 0.0 copy-start.10
  235.9 5.2 %fusion.40 = (bf16[1,256,1024]{2,1,0:T(8,128)(2,1)}, bf16[1,256,1024]{2,1,0:T(8,128)(2,1)}, bf16[1,256,1024]{2,1,0:T(8,128)(2,1)}, bf16[1,256,1024]{2,1,0:T(8,128)(2,1)}) fusion(bf16[1,256,1024]{2,1,0:T(8,128)(2,1)S(1)} %copy-done.6, bf16[1,256,1024]{2,1,0:T(8,128)(2,1)S(1)} %copy-done.12, bf16[1,256,1024]{2,1,0:T(8,128)(2,1)S(1)} %copy-done.7, ...), kind=kOutput, calls=%fused_computation.59 | convolution fusion | flops 1084489728 | bytes 11010048 | tf_op jit(solution)/shard_map/dot_general | solution.py:28
  241.2 0.0 copy-done.8
  241.2 0.0 copy-done.10
  241.2 10.5 %fusion.38 = (bf16[1,1024,256]{2,1,0:T(8,128)(2,1)}, bf16[1,1024,256]{2,1,0:T(8,128)(2,1)}, bf16[1,1024,256]{2,1,0:T(8,128)(2,1)}, bf16[1,1024,256]{2,1,0:T(8,128)(2,1)}) fusion(bf16[1,1024,256]{2,1,0:T(8,128)(2,1)S(1)} %copy-done.8, bf16[1,1024,256]{2,1,0:T(8,128)(2,1)S(1)} %copy-done.9, bf16[1,1024,256]{2,1,0:T(8,128)(2,1)S(1)} %copy-done.10, ...), kind=kOutput, calls=%fused_computation.57 | convolution fusion | flops 2170290176 | bytes 15736832 | tf_op jit(solution)/shard_map/dot_general | solution.py:28
  (3 shorter events, 0.0 us)
Async XLA Ops:
  0.6 8.3 %copy-start.4 = (s32[1,16,128]{2,1,0:T(8,128)S(1)}, s32[1,16,128]{2,1,0:T(8,128)}, u32[]{:S(2)}) copy-start(s32[1,16,128]{2,1,0:T(8,128)} %param.11) | copy-start | bytes 24580
  9.0 10.1 %copy-start = (bf16[1,1,128,1024]{3,2,1,0:T(8,128)(2,1)S(1)}, bf16[1,1,128,1024]{3,2,1,0:T(8,128)(2,1)}, u32[]{:S(2)}) copy-start(bf16[1,1,128,1024]{3,2,1,0:T(8,128)(2,1)} %param.21) | copy-start | bytes 786436
  9.0 10.1 %copy-start.1 = (bf16[1,256,1024]{2,1,0:T(8,128)(2,1)S(1)}, bf16[1,256,1024]{2,1,0:T(8,128)(2,1)}, u32[]{:S(2)}) copy-start(bf16[1,256,1024]{2,1,0:T(8,128)(2,1)} %param.16) | copy-start | bytes 1572868
  9.0 10.1 %copy-start.2 = (bf16[1,1024,256]{2,1,0:T(8,128)(2,1)S(1)}, bf16[1,1024,256]{2,1,0:T(8,128)(2,1)}, u32[]{:S(2)}) copy-start(bf16[1,1024,256]{2,1,0:T(8,128)(2,1)} %param.15) | copy-start | bytes 1572868
  19.1 59.2 %copy-start.9 = (bf16[1,1024,256]{2,1,0:T(8,128)(2,1)S(1)}, bf16[1,1024,256]{2,1,0:T(8,128)(2,1)}, u32[]{:S(2)}) copy-start(bf16[1,1024,256]{2,1,0:T(8,128)(2,1)} %param.13) | copy-start | bytes 1572868
  75.0 3.5 %copy-start.3 = (bf16[2048,1024]{1,0:T(8,128)(2,1)S(1)}, bf16[2048,1024]{1,0:T(8,128)(2,1)}, u32[]{:S(2)}) copy-start(bf16[2048,1024]{1,0:T(8,128)(2,1)} %get-tuple-element.17) | copy-start | bytes 12582916
  78.5 1.3 copy-start.11
  79.8 3.5 %copy-start.13 = (f32[2048,256]{1,0:T(8,128)}, f32[2048,256]{1,0:T(8,128)S(1)}, u32[]{:S(2)}) copy-start(f32[2048,256]{1,0:T(8,128)S(1)} %fusion.18) | copy-start | bytes 6291460
  84.3 61.8 %copy-start.5 = (bf16[16,128,1024]{2,1,0:T(8,128)(2,1)S(1)}, bf16[16,128,1024]{2,1,0:T(8,128)(2,1)}, u32[]{:S(2)}) copy-start(bf16[16,128,1024]{2,1,0:T(8,128)(2,1)} %get-tuple-element.18) | copy-start | bytes 12582916
  155.9 80.0 %copy-start.6 = (bf16[1,256,1024]{2,1,0:T(8,128)(2,1)S(1)}, bf16[1,256,1024]{2,1,0:T(8,128)(2,1)}, u32[]{:S(2)}) copy-start(bf16[1,256,1024]{2,1,0:T(8,128)(2,1)} %param.18) | copy-start | bytes 1572868
  155.9 80.0 %copy-start.7 = (bf16[1,256,1024]{2,1,0:T(8,128)(2,1)S(1)}, bf16[1,256,1024]{2,1,0:T(8,128)(2,1)}, u32[]{:S(2)}) copy-start(bf16[1,256,1024]{2,1,0:T(8,128)(2,1)} %param.20) | copy-start | bytes 1572868
  155.9 80.0 %copy-start.12 = (bf16[1,256,1024]{2,1,0:T(8,128)(2,1)S(1)}, bf16[1,256,1024]{2,1,0:T(8,128)(2,1)}, u32[]{:S(2)}) copy-start(bf16[1,256,1024]{2,1,0:T(8,128)(2,1)} %param.14) | copy-start | bytes 1572868
  155.9 80.0 %copy-start.14 = (f32[2048,256]{1,0:T(8,128)S(1)}, f32[2048,256]{1,0:T(8,128)}, u32[]{:S(2)}) copy-start(f32[2048,256]{1,0:T(8,128)} %copy-done.13) | copy-start | bytes 6291460
  235.9 5.3 %copy-start.8 = (bf16[1,1024,256]{2,1,0:T(8,128)(2,1)S(1)}, bf16[1,1024,256]{2,1,0:T(8,128)(2,1)}, u32[]{:S(2)}) copy-start(bf16[1,1024,256]{2,1,0:T(8,128)(2,1)} %param.17) | copy-start | bytes 1572868
  235.9 5.2 %copy-start.10 = (bf16[1,1024,256]{2,1,0:T(8,128)(2,1)S(1)}, bf16[1,1024,256]{2,1,0:T(8,128)(2,1)}, u32[]{:S(2)}) copy-start(bf16[1,1024,256]{2,1,0:T(8,128)(2,1)} %param.19) | copy-start | bytes 1572868

commit v2 on v0

v2 whole, which is shorter than its diff:
```python
import functools

import jax
import jax.numpy as jnp
from jax import lax
from jax.experimental import pallas as pl
from jax.experimental.pallas import tpu as pltpu
from jax.sharding import PartitionSpec as P

epsilon = 1e-06
momentum_decay = 0.9
outer_rate = 0.7
inner_rate = 0.01
MESH = pl.DeviceIdType.MESH
RING = 4
PATHS = 16
TOKENS = 128
GROUPS = 2
PART = TOKENS // GROUPS
ROWS = PATHS * PART
LAG = 9
CHUNK = 256
f32, b16 = jnp.float32, jnp.bfloat16


def outer_update(parameter, moment, gradient, sharers):
    average = gradient / sharers
    new_moment = momentum_decay * moment.astype(f32) + average
    new_parameter = parameter.astype(f32) - outer_rate * inner_rate * (
        average + momentum_decay * new_moment
    )
    return (new_parameter.astype(b16)[None], new_moment.astype(b16)[None])


def gelu_and_slope(v):
    scale, cubic = 0.7978845608028654, 0.044715
    square = v * v
    t = jnp.tanh(scale * v * (1.0 + cubic * square))
    half = 0.5 * (1.0 + t)
    slope = half + 0.5 * v * (1.0 - t * t) * (scale * (1.0 + 3.0 * cubic * square))
    return v * half, slope


def dot(a, b):
    return jnp.dot(a, b, preferred_element_type=f32)


def dot_rows(a, b):
    return lax.dot_general(a, b, (((0,), (0,)), ((), ())), preferred_element_type=f32)


def dot_cols(a, b):
    return lax.dot_general(a, b, (((1,), (1,)), ((), ())), preferred_element_type=f32)


class Place:
    def __init__(self):
        row, col = lax.axis_index("row"), lax.axis_index("col")
        self.zl, self.x = row // 4, row % 4
        self.zh, self.y, self.k = col // 8, (col // 2) % 4, col % 2
        self.stay = (self.zl // 2) == self.k
        other_zl = (self.zl + 2) % 4
        self.swap = (other_zl * 4 + self.x, self.zh * 8 + self.y * 2 + (1 - self.k))


class ColGroup:
    def __init__(self, place):
        self.place = place
        self.p, self.t, self.k = place.zh, place.y, place.k

    def device(self, p, t, k):
        return (self.place.zl * 4 + self.place.x, p * 8 + t * 2 + k)


class RowGroup:
    def __init__(self, place):
        self.place = place
        self.p, self.t, self.k = place.zl % 2, place.x, place.k
        self.half = place.zl // 2

    def device(self, p, t, k):
        return ((self.half * 2 + p) * 4 + t, self.place.zh * 8 + self.place.y * 2 + k)


def slot(p, t, k):
    return k * 8 + p * 4 + t


def first_row(g, p, t, k):
    return pl.multiple_of((g * PATHS + slot(p, t, k)) * PART, PART)


def near(group):
    p, t, k = group.p, group.t, group.k
    up, down = (t + 1) % RING, (t + RING - 1) % RING
    return {
        "pair": group.device(1 - p, t, k),
        "sibling": group.device(p, t, 1 - k),
        "up": group.device(p, up, k),
        "down": group.device(p, down, k),
    }


def greet(devices):
    barrier = pltpu.get_barrier_semaphore()
    for device in devices:
        pl.semaphore_signal(barrier, inc=1, device_id=device, device_id_type=MESH)
    pl.semaphore_wait(barrier, len(devices))


class Mail:
    def __init__(self, send_sem, recv_sem):
        self.send_sem, self.recv_sem = send_sem, recv_sem
        self.sent = []
        self.used = 0

    def take(self, count):
        self.used += count
        return self.used - count

    def copy(self, number, src, dst, device):
        return pltpu.make_async_remote_copy(
            src_ref=src,
            dst_ref=dst,
            send_sem=self.send_sem.at[number],
            recv_sem=self.recv_sem.at[number],
            device_id=device,
            device_id_type=MESH,
        )

    def send(self, number, src, dst, device):
        copy = self.copy(number, src, dst, device)
        copy.start()
        self.sent.append(copy)

    def arrived(self, number, ref, device):
        self.copy(number, ref, ref, device).wait_recv()

    def finish(self):
        for copy in self.sent:
            copy.wait_send()
        self.sent = []


class Gather:
    def __init__(self, group, mail, region, half):
        self.g, self.mail, self.region, self.half = group, mail, region, half
        self.base = mail.take(17)
        self.peers = near(group)

    def send(self, m, ref, to):
        self.mail.send(self.base + m, ref, ref, self.peers[to])

    def got(self, m, ref):
        self.mail.arrived(self.base + m, ref, self.peers["sibling"])

    def steps(self):
        g = self.g
        p, t, k = g.p, g.t, g.k
        before, after, far = (t + RING - 1) % RING, (t + 1) % RING, (t + 2) % RING
        own = self.region(p, t, k)
        self.send(0, own, "pair")
        self.send(2, own, "up")
        self.send(3, own, "down")
        self.send(1, own, "sibling")
        yield
        for q, first, fwd in ((p, 2, 7), (1 - p, 4, 11)):
            if first == 4:
                ref = self.region(q, t, k)
                self.got(0, ref)
                self.send(4, ref, "up")
                self.send(5, ref, "down")
                self.send(6, ref, "sibling")
                yield
            ref = self.region(q, before, k)
            self.got(first, ref)
            self.send(fwd, self.half(q, before, k, 0), "up")
            self.send(fwd + 1, ref, "sibling")
            ref = self.region(q, after, k)
            self.got(first + 1, ref)
            self.send(fwd + 2, self.half(q, after, k, 1), "down")
            self.send(fwd + 3, ref, "sibling")
            yield
        for q, fwd, last in ((p, 7, 15), (1 - p, 11, 16)):
            self.got(fwd, self.half(q, far, k, 0))
            self.got(fwd + 2, self.half(q, far, k, 1))
            self.send(last, self.region(q, far, k), "sibling")
            yield
        for m, q, s in (
            (1, p, t),
            (6, 1 - p, t),
            (8, p, before),
            (10, p, after),
            (12, 1 - p, before),
            (14, 1 - p, after),
            (15, p, far),
            (16, 1 - p, far),
        ):
            self.got(m, self.region(q, s, 1 - k))


def token_regions(buf, g):
    def region(p, t, k):
        return buf.at[pl.ds(first_row(g, p, t, k), PART)]

    def half(p, t, k, h):
        return buf.at[pl.ds(first_row(g, p, t, k) + h * (PART // 2), PART // 2)]

    return region, half


def add_rows(dst, at, left, left_at, right, right_at, count):
    step = 16

    def body(i, _):
        off = i * step
        dst[pl.ds(at + off, step)] = (
            left[pl.ds(left_at + off, step)].astype(f32)
            + right[pl.ds(right_at + off, step)].astype(f32)
        ).astype(b16)
        return 0

    lax.fori_loop(0, count // step, body, 0, unroll=2)


class Scatter:
    def __init__(self, group, mail, g, part, bufs, out):
        self.g, self.mail, self.n, self.part, self.out = group, mail, g, part, out
        self.base = mail.take(2 + 4 + 8 + 1)
        self.from_sibling, self.sums, self.from_far, self.from_near, self.from_pair = bufs
        self.peers = near(group)

    def steps(self):
        group, mail, part, n = self.g, self.mail, self.part, self.n
        from_sibling, sums, from_far, from_near, from_pair = (
            self.from_sibling.at[n],
            self.sums.at[n],
            self.from_far.at[n],
            self.from_near.at[n],
            self.from_pair.at[n],
        )
        p, t, k = group.p, group.t, group.k
        peers = self.peers
        half = PART // 2
        side = {1: 1 - p, 0: p}
        sib, far, nearby, pair = self.base, self.base + 2, self.base + 6, self.base + 14

        def cell(q, s):
            return pl.multiple_of((side[q] * 4 + (t + s) % RING) * PART, PART)

        def got(number, ref):
            mail.arrived(number, ref, peers["sibling"])

        for q in (1, 0):
            four = pl.ds(pl.multiple_of(side[q] * 4 * PART, 4 * PART), 4 * PART)
            src = part.at[pl.ds(first_row(n, side[q], 0, 1 - k), 4 * PART)]
            mail.send(sib + q, src, from_sibling.at[four], peers["sibling"])
        yield

        def chip_sum(q, s):
            own = first_row(n, side[q], (t + s) % RING, k)
            add_rows(sums, cell(q, s), part, own, from_sibling, cell(q, s), PART)

        for q in (1, 0):
            four = pl.ds(pl.multiple_of(side[q] * 4 * PART, 4 * PART), 4 * PART)
            got(sib + q, from_sibling.at[four])
            chip_sum(q, 2)
            c = cell(q, 2)
            mail.send(far + 2 * q, sums.at[pl.ds(c, half)], from_far.at[2 * q], peers["up"])
            mail.send(
                far + 2 * q + 1, sums.at[pl.ds(c + half, half)], from_far.at[2 * q + 1], peers["down"]
            )
            chip_sum(q, 1)
            low = pl.ds(cell(q, 1) + half, half)
            mail.send(
                nearby + 4 * q, sums.at[low], from_near.at[2 * q, pl.ds(half, half)], peers["up"]
            )
            chip_sum(q, 3)
            top = pl.ds(cell(q, 3), half)
            mail.send(
                nearby + 4 * q + 1, sums.at[top], from_near.at[2 * q + 1, pl.ds(0, half)], peers["down"]
            )
        for q in (1, 0):
            chip_sum(q, 0)
        yield
        for q in (1, 0):
            got(far + 2 * q, from_far.at[2 * q])
            c = cell(q, 1)
            add_rows(sums, c, sums, c, from_far.at[2 * q], 0, half)
            mail.send(
                nearby + 4 * q + 2,
                sums.at[pl.ds(c, half)],
                from_near.at[2 * q, pl.ds(0, half)],
                peers["up"],
            )
            got(far + 2 * q + 1, from_far.at[2 * q + 1])
            c = pl.multiple_of(cell(q, 3) + half, half)
            add_rows(sums, c, sums, c, from_far.at[2 * q + 1], 0, half)
            mail.send(
                nearby + 4 * q + 3,
                sums.at[pl.ds(c, half)],
                from_near.at[2 * q + 1, pl.ds(half, half)],
                peers["down"],
            )
            yield

        def wait_near(q):
            got(nearby + 4 * q, from_near.at[2 * q, pl.ds(half, half)])
            got(nearby + 4 * q + 1, from_near.at[2 * q + 1, pl.ds(0, half)])
            got(nearby + 4 * q + 2, from_near.at[2 * q, pl.ds(0, half)])
            got(nearby + 4 * q + 3, from_near.at[2 * q + 1, pl.ds(half, half)])

        def total(q, i):
            rows = pl.ds(i * 16, 16)
            return (
                sums[pl.ds(cell(q, 0) + i * 16, 16)].astype(f32)
                + from_near[2 * q, rows].astype(f32)
                + from_near[2 * q + 1, rows].astype(f32)
            )

        wait_near(1)

        def pair_part(i, _):
            sums[pl.ds(cell(1, 0) + i * 16, 16)] = total(1, i).astype(b16)
            return 0

        lax.fori_loop(0, PART // 16, pair_part, 0)
        mail.send(pair, sums.at[pl.ds(cell(1, 0), PART)], from_pair, peers["pair"])
        yield
        wait_near(0)
        yield
        got(pair, from_pair)

        def own_part(i, _):
            rows = pl.ds(i * 16, 16)
            self.out[rows] = (total(0, i) + from_pair[rows].astype(f32)).astype(self.out.dtype)
            return 0

        lax.fori_loop(0, PART // 16, own_part, 0)


def scatter_scratch(width):
    return [
        pltpu.VMEM((GROUPS, 8 * PART, width), b16),
        pltpu.VMEM((GROUPS, 8 * PART, width), b16),
        pltpu.VMEM((GROUPS, 4, PART // 2, width), b16),
        pltpu.VMEM((GROUPS, 4, PART, width), b16),
        pltpu.VMEM((GROUPS, PART, width), b16),
    ]


class Swap:
    def __init__(self, place, mail):
        self.place, self.mail, self.number = place, mail, mail.take(1)

    def start(self, src, own_dst, swap_dst):
        self.src, self.dst = src, swap_dst

        @pl.when(self.place.stay)
        def _():
            own_dst[...] = src[...]

        @pl.when(jnp.logical_not(self.place.stay))
        def _():
            self.mail.copy(self.number, src, swap_dst, self.place.swap).start()

    def wait(self):
        @pl.when(jnp.logical_not(self.place.stay))
        def _():
            self.mail.copy(self.number, self.src, self.dst, self.place.swap).wait()


def whole_step(
    pieces, cot, up_one, down_one, up_two, down_two,
    grad_up_one, grad_down_one, grad_up_two, grad_down_two,
    wide, other, inputs, normed_one, slope_one, act_one, part_one,
    cots, up_home, down_home, mixed, middle, mine, normed_two, act_two, slope_two, part_two,
    sum_up_two, sum_down_two, ready_up_two, ready_down_two, back_mine, back, group,
    *scratch,
):
    col_bufs, row_bufs, (send_sem, recv_sem) = scratch[:5], scratch[5:10], scratch[10:]
    place = Place()
    col, row = ColGroup(place), RowGroup(place)
    mail = Mail(send_sem, recv_sem)
    peers_c, peers_r = near(col), near(row)
    greet(
        [peers_c["sibling"], peers_c["pair"], peers_c["up"], peers_c["down"]]
        + [peers_r["pair"], peers_r["up"], peers_r["down"], place.swap]
    )
    k = place.k
    half_rows = ROWS // 2
    my_row = functools.partial(first_row, p=row.p, t=row.t, k=row.k)
    swap_row = functools.partial(first_row, p=row.p, t=row.t, k=1 - row.k)

    def normal_factor(values):
        return lax.rsqrt(jnp.mean(values * values, axis=-1, keepdims=True) + epsilon)

    def rows_of(g, i):
        return pl.ds(pl.multiple_of(g * ROWS + i * CHUNK, CHUNK), CHUNK)

    def accumulate(ref, fresh, value):
        if fresh is True:
            ref[...] = value
        elif fresh is False:
            ref[...] += value

    def chunks(body):
        lax.fori_loop(0, ROWS // CHUNK, lambda i, c: (body(i), c)[1], 0)

    def level_one(g):
        def body(i):
            rows = rows_of(g, i)
            values = inputs[rows].astype(f32)
            normed = (values * normal_factor(values)).astype(b16)
            normed_one[rows] = normed
            act, slope = gelu_and_slope(dot(normed, up_one[...]))
            slope_one[rows] = slope
            act = act.astype(b16)
            act_one[rows] = act
            part_one[rows] = dot(act, down_one[...]).astype(b16)

        chunks(body)

    def level_two(g):
        def body(i):
            rows = rows_of(g, i)
            act, slope = gelu_and_slope(dot(normed_two[rows], up_home[...]))
            act_two[rows] = act.astype(b16)
            slope = (slope * dot_cols(cots[rows], down_home[...])).astype(b16)
            slope_two[rows] = slope
            part_two[rows] = dot_cols(slope, up_home[...]).astype(b16)

        chunks(body)

    def level_two_grads(g):
        def body(i):
            rows = rows_of(g, i)
            sum_down_two[...] += dot_rows(act_two[rows], cots[rows])
            sum_up_two[...] += dot_rows(slope_two[rows], normed_two[rows])

        chunks(body)

    def level_one_back(g):
        def body(i):
            rows = rows_of(g, i)
            upstream = group[rows]
            grad_down_one[...] += dot_rows(act_one[rows], upstream)
            slope = (slope_one[rows] * dot_cols(upstream, down_one[...])).astype(b16)
            grad_up_one[...] += dot_rows(slope, normed_one[rows])

        chunks(body)

    swaps = {name: Swap(place, mail) for name in ("cot", "up", "down", "grad_up", "grad_down")}

    def chain(g):
        number = mail.take(1)
        own = pieces[pl.ds(g * ROWS, ROWS)]
        wide[pl.ds(g * ROWS, ROWS)] = jnp.concatenate([own, own], axis=1)
        there = pl.ds(pl.multiple_of(g * ROWS + (1 - k) * half_rows, half_rows), half_rows)
        here = pl.ds(pl.multiple_of(g * ROWS + k * half_rows, half_rows), half_rows)
        landed = other.at[pl.ds(g * half_rows, half_rows)]
        mail.send(number, wide.at[there], landed, peers_c["sibling"])
        yield
        mail.arrived(number, landed, peers_c["sibling"])
        lane = lax.broadcasted_iota(jnp.int32, (half_rows, 128), 1) // 64

        def lanes(p, t):
            return pl.ds(pl.multiple_of((p * 4 + t) * 128, 128), 128)

        inputs[here, lanes(col.p, col.t)] = jnp.where(lane == k, wide[here], landed[...])

        def region(p, t, k):
            at = pl.multiple_of(g * ROWS + k * half_rows, half_rows)
            return inputs.at[pl.ds(at, half_rows), lanes(p, t)]

        def half(p, t, k, h):
            quarter = half_rows // 2
            at = pl.multiple_of(g * ROWS + k * half_rows + h * quarter, quarter)
            return inputs.at[pl.ds(at, quarter), lanes(p, t)]

        yield from Gather(col, mail, region, half).steps()
        level_one(g)
        yield from Scatter(col, mail, g, part_one, col_bufs, mixed).steps()
        own_input = inputs[pl.ds(first_row(g, col.p, col.t, col.k), PART)]
        values = own_input.astype(f32) + mixed[...]
        middle[g] = values
        mine[g] = (values * normal_factor(values)).astype(b16)
        swap = Swap(place, mail)
        swap.start(
            mine.at[g],
            normed_two.at[pl.ds(my_row(g), PART)],
            normed_two.at[pl.ds(swap_row(g), PART)],
        )
        yield
        swap.wait()
        yield from Gather(row, mail, *token_regions(normed_two, g)).steps()
        if g == 0:
            swaps["up"].wait()
            swaps["down"].wait()
        level_two(g)
        scatter = Scatter(row, mail, g, part_two, row_bufs, back_mine.at[g]).steps()
        next(scatter)
        yield
        next(scatter)
        level_two_grads(g)
        yield
        if g == GROUPS - 1:
            ready_up_two[...] = sum_up_two[...].astype(b16)
            ready_down_two[...] = sum_down_two[...].astype(b16)
            swaps["grad_up"].start(ready_up_two, grad_up_two, grad_up_two)
            swaps["grad_down"].start(ready_down_two, grad_down_two, grad_down_two)
        yield from scatter
        swap = Swap(place, mail)
        swap.start(back_mine.at[g], back.at[g], back.at[g])
        yield
        swap.wait()
        upstream = back[g].astype(f32)
        values = middle[g]
        factor = normal_factor(values)
        through = factor * upstream - values * (factor * factor * factor) * jnp.mean(
            upstream * values, axis=-1, keepdims=True
        )
        own_cot = cot[pl.ds(g * PART, PART)].astype(f32)
        group[pl.ds(first_row(g, col.p, col.t, col.k), PART)] = (own_cot + through).astype(b16)
        yield from Gather(col, mail, *token_regions(group, g)).steps()
        level_one_back(g)

    def background():
        for ref in (grad_up_one, grad_down_one, sum_up_two, sum_down_two):
            ref[...] = jnp.zeros_like(ref)
        cot_swaps = [Swap(place, mail) for _ in range(GROUPS)]
        for g, swap in enumerate(cot_swaps):
            swap.start(
                cot.at[pl.ds(g * PART, PART)],
                cots.at[pl.ds(my_row(g), PART)],
                cots.at[pl.ds(swap_row(g), PART)],
            )
        yield
        swaps["up"].start(up_two, up_home, up_home)
        swaps["down"].start(down_two, down_home, down_home)
        for g, swap in enumerate(cot_swaps):
            swap.wait()
        gathers = [Gather(row, mail, *token_regions(cots, g)).steps() for g in range(GROUPS)]
        while gathers:
            gathers = [gather for gather in gathers if next(gather, "done") != "done"]
            yield

    tasks = [(0, chain(0)), (1, background())] + [(LAG * g, chain(g)) for g in range(1, GROUPS)]
    tick = 0
    while tasks:
        left = []
        for begin, task in tasks:
            if tick < begin or next(task, "done") != "done":
                left.append((begin, task))
        tasks = left
        tick += 1
    swaps["grad_up"].wait()
    swaps["grad_down"].wait()
    mail.finish()


def on_device(
    token_ids,
    embedding,
    up_one,
    down_one,
    up_two,
    down_two,
    moment_up_one,
    moment_down_one,
    moment_up_two,
    moment_down_two,
    cotangent,
):
    sharers = PATHS
    width, hidden = up_one.shape[1:]
    ids = token_ids[0].reshape(2, 4, 2, GROUPS, PART).transpose(3, 2, 0, 1, 4).reshape(-1)
    count = ids.shape[0]
    pieces = embedding.at[ids].get(mode="promise_in_bounds")
    vmem = pl.BlockSpec(memory_space=pltpu.VMEM)
    args = [pieces, cotangent[0, 0], up_one[0], down_one[0], up_two[0], down_two[0]]
    out_shape = [jax.ShapeDtypeStruct((hidden, width), f32)] * 2
    out_shape += [jax.ShapeDtypeStruct((hidden, width), b16)] * 2
    tokens_b16 = pltpu.VMEM((count, width), b16)
    part_b16 = pltpu.VMEM((GROUPS, PART, width), b16)
    hidden_b16 = pltpu.VMEM((count, hidden), b16)
    grad_f32 = pltpu.VMEM((hidden, width), f32)
    grad_b16 = pltpu.VMEM((hidden, width), b16)
    scratch = [
        pltpu.VMEM((count, 128), b16),
        pltpu.VMEM((count // 2, 128), b16),
        tokens_b16,
        tokens_b16,
        pltpu.VMEM((count, hidden), f32),
        hidden_b16,
        tokens_b16,
        tokens_b16,
        pltpu.VMEM((width, hidden), b16),
        pltpu.VMEM((hidden, width), b16),
        pltpu.VMEM((PART, width), f32),
        pltpu.VMEM((GROUPS, PART, width), f32),
        part_b16,
        tokens_b16,
        hidden_b16,
        hidden_b16,
        tokens_b16,
        grad_f32,
        grad_f32,
        grad_b16,
        grad_b16,
        part_b16,
        part_b16,
        tokens_b16,
    ]
    scratch += scatter_scratch(width) + scatter_scratch(width)
    messages = GROUPS * (1 + 17 + 15 + 1 + 17 + 15 + 1 + 17 + 1 + 17) + 5
    scratch += [pltpu.SemaphoreType.DMA((messages,)), pltpu.SemaphoreType.DMA((messages,))]
    grad_up_one, grad_down_one, grad_up_two, grad_down_two = pl.pallas_call(
        whole_step,
        name="whole_step",
        out_shape=out_shape,
        in_specs=[vmem] * len(args),
        out_specs=[vmem] * len(out_shape),
        scratch_shapes=scratch,
        compiler_params=pltpu.CompilerParams(
            collective_id=0, has_side_effects=True, vmem_limit_bytes=60 * 2**20
        ),
    )(*args)
    new_up_one, new_moment_up_one = outer_update(
        up_one[0], moment_up_one[0], grad_up_one.T, sharers
    )
    new_down_one, new_moment_down_one = outer_update(
        down_one[0], moment_down_one[0], grad_down_one, sharers
    )
    new_up_two, new_moment_up_two = outer_update(
        up_two[0], moment_up_two[0], grad_up_two.T.astype(f32), sharers
    )
    new_down_two, new_moment_down_two = outer_update(
        down_two[0], moment_down_two[0], grad_down_two.astype(f32), sharers
    )
    return (
        new_up_one,
        new_down_one,
        new_up_two,
        new_down_two,
        new_moment_up_one,
        new_moment_down_one,
        new_moment_up_two,
        new_moment_down_two,
    )


def solution(mesh):
    in_specs = (
        P("row", None, None),
        P(None, "col"),
        P("row", None, "col"),
        P("row", "col", None),
        P("col", None, "row"),
        P("col", "row", None),
        P("row", None, "col"),
        P("row", "col", None),
        P("col", None, "row"),
        P("col", "row", None),
        P("row", "col", None, None),
    )
    out_specs = (
        P("row", None, "col"),
        P("row", "col", None),
        P("col", None, "row"),
        P("col", "row", None),
        P("row", None, "col"),
        P("row", "col", None),
        P("col", None, "row"),
        P("col", "row", None),
    )
    return jax.shard_map(
        on_device, mesh=mesh, in_specs=in_specs, out_specs=out_specs, check_vma=False
    )
```

time: 595 us -> 225 us (0.38)
  waiting for transfers between devices: 506 us -> 0 us
  Pallas kernels: 0 us -> 190 us
  matrix products: 40.9 us -> 0 us
  between operations: 14.3 us -> 0.77 us
  local copies, waits for them, and re-layouts: 22 us -> 28.2 us
    all_gather x4 -> x0, waiting for transfers between devices: 318 us -> none  [the longest x1 83.5 us: on_device(): lax.all_gather(own_cot, 'row', axis=0, tiled=True)]
    pallas_call x0 -> x1, Pallas kernels: none -> 190 us  [on_device(): pl.pallas_call(whole_step, name='whole_step', out_shape=out_shape, in_spe...]
    reduce_scatter x2 -> x0, waiting for transfers between devices: 188 us -> none  [the longest x1 96.9 us: on_device(): lax.psum_scatter(jnp.dot(block, down_one[0], preferred_element_type=jnp.f...]
    dot_general x9 -> x0, matrix products: 40.9 us -> none  [the longest x4 22.8 us: contract_rows(): lax.dot_general(first_operand, second_operand, (((0,), (0,)), ((), ())),...]
    unnamed x34 -> x23, local copies, waits for them, and re-layouts: 10.1 us -> 15.8 us
  transfers between devices with their start and end apart: 6 -> 0, of which waited for: 6 -> 0; matrix products, arithmetic and copies ran while one was open for 2% -> 0% of each run, Pallas kernels for 0% -> 0%
where the time goes in v2:
time: 225 us; the launch traced here: 224 us
  Pallas kernels  190 us (84%)
  local copies, waits for them, and re-layouts  28.2 us (13%)
  other arithmetic  5.93 us (3%)
    pallas_call x1, Pallas kernels, on_device(): pl.pallas_call(whole_step, name='whole_step', out_shape=out_shape, in_spe...  190 us
    unnamed x23, local copies, waits for them, and re-layouts  15.8 us
    gather x1, local copies, waits for them, and re-layouts, on_device(): pieces = embedding.at[ids].get(mode='promise_in_bounds')  12.2 us
    broadcast_in_dim x2, other arithmetic, outer_update(): return (new_parameter.astype(b16)[None], new_moment.astype(b16)[None])  5.91 us

profile of v2, /device:TPU:1, one launch (start us, length us, event | category | flops | bytes accessed | tf_op | source)
XLA Modules:
  0.0 224.4 jit_solution(10422490889867421313)
XLA Ops:
  0.6 0.0 copy-start.6
  0.6 0.0 copy-start.2
  0.7 0.0 copy-start.3
  0.7 0.0 copy-start.5
  0.7 8.4 %copy.32 = bf16[32000,64]{1,0:T(8,128)(2,1)} copy(bf16[32000,64]{0,1:T(8,128)(2,1)} %param.12) | data formatting | bytes 8192000 | tf_op args[1]
  9.0 0.0 copy-done.6
  9.0 0.0 copy-start
  9.0 0.0 copy-start.1
  9.0 0.0 copy-start.4
  9.1 0.1 reshape_squeeze.3
  9.1 0.1 reshape.59
  9.3 12.2 %gather_fusion = bf16[2048,64]{1,0:T(8,128)(2,1)} fusion(bf16[32000,64]{1,0:T(8,128)(2,1)} %copy.32, s32[2048]{0:T(1024)S(1)} %broadcast_clamp_fusion), kind=kCustom, calls=%fused_computation | custom fusion | bytes 532480 | tf_op jit(solution)/shard_map/gather | solution.py:579
  21.5 189.5 %whole_step.1 = (f32[256,1024]{1,0:T(8,128)}, f32[256,1024]{1,0:T(8,128)}, bf16[256,1024]{1,0:T(8,128)(2,1)}, bf16[256,1024]{1,0:T(8,128)(2,1)}) custom-call(bf16[2048,64]{1,0:T(8,128)(2,1)} %gather_fusion, bf16[128,1024]{1,0:T(8,128)(2,1)} %bitcast.109, bf16[1024,256]{1,0:T(8,128)(2,1)} %bitcast.105, bf16[256,1024]{1,0:T(8,128)(2,1)} %bitcast.107, ...), custom_call_target="tpu_custom_call" | custom-call | tf_op jit(solution)/shard_map/whole_step/pallas_call | solution.py:618
  211.0 0.0 copy-done.2
  211.0 0.0 copy-done.3
  211.0 0.0 copy-done.5
  211.0 3.4 %fusion.11 = (bf16[1,256,1024]{2,1,0:T(8,128)(2,1)}, bf16[1,256,1024]{2,1,0:T(8,128)(2,1)}, bf16[1,256,1024]{2,1,0:T(8,128)(2,1)}, bf16[1,256,1024]{2,1,0:T(8,128)(2,1)}) fusion(f32[256,1024]{1,0:T(8,128)} %get-tuple-element.13, bf16[1,256,1024]{2,1,0:T(8,128)(2,1)S(1)} %copy-done.5, bf16[1,256,1024]{2,1,0:T(8,128)(2,1)S(1)} %copy-done.2, ...), kind=kLoop, calls=%fused_computation.22 | loop fusion | flops 6029312 | bytes 5767168 | tf_op jit(solution)/shard_map/broadcast_in_dim | solution.py:32
  214.5 0.0 copy-done
  214.5 0.2 copy.30
  214.7 0.0 copy-done.1
  214.7 0.2 copy.33
  214.9 0.0 copy-done.4
  214.9 1.0 copy.36
  215.9 2.0 copy.37
  217.9 2.5 %fusion.10 = (bf16[1,1024,256]{1,2,0:T(8,128)(2,1)S(1)}, bf16[1,1024,256]{1,2,0:T(8,128)(2,1)S(1)}, bf16[1,1024,256]{1,2,0:T(8,128)(2,1)S(1)}, bf16[1,1024,256]{1,2,0:T(8,128)(2,1)S(1)}) fusion(f32[256,1024]{1,0:T(8,128)} %get-tuple-element.12, bf16[1,1024,256]{1,2,0:T(8,128)(2,1)} %copy.36, bf16[1,1024,256]{1,2,0:T(8,128)(2,1)S(1)} %copy.30, ...), kind=kLoop, calls=%fused_computation.21 | loop fusion | flops 6029312 | bytes 5767168 | tf_op jit(solution)/shard_map/broadcast_in_dim | solution.py:32
  220.4 1.0 copy.38
  221.4 1.0 copy.39
  222.4 1.0 copy.40
  223.4 1.0 copy.41
  (3 shorter events, 0.0 us)
Async XLA Ops:
  0.6 8.4 %copy-start.6 = (s32[1,16,128]{2,1,0:T(8,128)S(1)}, s32[1,16,128]{2,1,0:T(8,128)}, u32[]{:S(2)}) copy-start(s32[1,16,128]{2,1,0:T(8,128)} %param.11) | copy-start | bytes 24580
  0.6 210.3 %copy-start.2 = (bf16[1,256,1024]{2,1,0:T(8,128)(2,1)S(1)}, bf16[1,256,1024]{2,1,0:T(8,128)(2,1)}, u32[]{:S(2)}) copy-start(bf16[1,256,1024]{2,1,0:T(8,128)(2,1)} %param.14) | copy-start | bytes 1572868
  0.7 210.3 %copy-start.3 = (bf16[1,256,1024]{2,1,0:T(8,128)(2,1)S(1)}, bf16[1,256,1024]{2,1,0:T(8,128)(2,1)}, u32[]{:S(2)}) copy-start(bf16[1,256,1024]{2,1,0:T(8,128)(2,1)} %param.16) | copy-start | bytes 1572868
  0.7 210.3 %copy-start.5 = (bf16[1,256,1024]{2,1,0:T(8,128)(2,1)S(1)}, bf16[1,256,1024]{2,1,0:T(8,128)(2,1)}, u32[]{:S(2)}) copy-start(bf16[1,256,1024]{2,1,0:T(8,128)(2,1)} %param.18) | copy-start | bytes 1572868
  9.0 205.4 %copy-start = (bf16[1,1024,256]{2,1,0:T(8,128)(2,1)S(1)}, bf16[1,1024,256]{2,1,0:T(8,128)(2,1)}, u32[]{:S(2)}) copy-start(bf16[1,1024,256]{2,1,0:T(8,128)(2,1)} %param.13) | copy-start | bytes 1572868
  9.0 205.6 %copy-start.1 = (bf16[1,1024,256]{2,1,0:T(8,128)(2,1)S(1)}, bf16[1,1024,256]{2,1,0:T(8,128)(2,1)}, u32[]{:S(2)}) copy-start(bf16[1,1024,256]{2,1,0:T(8,128)(2,1)} %param.15) | copy-start | bytes 1572868
  9.0 205.8 %copy-start.4 = (bf16[1,1024,256]{2,1,0:T(8,128)(2,1)S(1)}, bf16[1,1024,256]{2,1,0:T(8,128)(2,1)}, u32[]{:S(2)}) copy-start(bf16[1,1024,256]{2,1,0:T(8,128)(2,1)} %param.17) | copy-start | bytes 1572868

commit v3 on v2

--- a/solution.py
+++ b/solution.py
@@ -18,18 +18,59 @@
 GROUPS = 2
 PART = TOKENS // GROUPS
 ROWS = PATHS * PART
-LAG = 9
+ORDER = (
+    0, 1, 2, 2, 0, 1, 2, 2, 0, 1, 0, 2, 2, 2, 1, 0, 0, 2, 1, 1, 2, 2, 0, 0, 1, 2, 2, 0, 0, 1,
+    0, 2, 0, 1, 1, 2, 0, 0, 1, 1, 0, 1, 1, 0, 0, 1, 0, 1, 0, 0, 1, 1, 0, 0, 1, 1, 0, 0, 1, 0,
+    1, 0, 0, 1, 1, 0, 1, 0, 1, 1, 0, 1, 1, 0, 0, 1, 0, 0, 1, 0, 1, 0, 1, 1, 1, 1,
+)
 CHUNK = 256
+COLLECTIVE = 0
+LATE = 2
 f32, b16 = jnp.float32, jnp.bfloat16
 
 
-def outer_update(parameter, moment, gradient, sharers):
-    average = gradient / sharers
-    new_moment = momentum_decay * moment.astype(f32) + average
-    new_parameter = parameter.astype(f32) - outer_rate * inner_rate * (
-        average + momentum_decay * new_moment
-    )
-    return (new_parameter.astype(b16)[None], new_moment.astype(b16)[None])
+def update_kernel(sharers, *refs):
+    grads, weights, moments, new_weights, new_moments = (refs[4 * i : 4 * i + 4] for i in range(5))
+    for i in range(4):
+        gradient = grads[i][...].astype(f32)
+        if i % 2 == 0:
+            gradient = gradient.T
+        average = gradient * (1.0 / sharers)
+        new_moment = momentum_decay * moments[i][...].astype(f32) + average
+        new_moments[i][0] = new_moment.astype(b16)
+        new_weights[i][0] = (
+            weights[i][...].astype(f32)
+            - outer_rate * inner_rate * (average + momentum_decay * new_moment)
+        ).astype(b16)
+
+
+def update(grads, weights, moments, sharers):
+    hidden, width = weights[1].shape
+    block = hidden // 2
+    up = pl.BlockSpec((width, block), lambda i: (0, i))
+    down = pl.BlockSpec((block, width), lambda i: (i, 0))
+    new_up = pl.BlockSpec((1, width, block), lambda i: (0, 0, i))
+    new_down = pl.BlockSpec((1, block, width), lambda i: (0, i, 0))
+    return pl.pallas_call(
+        functools.partial(update_kernel, sharers),
+        name="update",
+        grid=(2,),
+        out_shape=[jax.ShapeDtypeStruct((1,) + w.shape, b16) for w in weights] * 2,
+        in_specs=[down] * 4 + [up, down, up, down] * 2,
+        out_specs=[new_up, new_down, new_up, new_down] * 2,
+        compiler_params=pltpu.CompilerParams(vmem_limit_bytes=60 * 2**20),
+    )(*grads, *weights, *moments)
+
+
+def swap_pairs():
+    pairs = []
+    for zl in range(4):
+        for x in range(4):
+            for col in range(16):
+                if zl // 2 != col % 2:
+                    source = (zl * 4 + x) * 16 + col
+                    pairs.append((source, ((zl + 2) % 4 * 4 + x) * 16 + (col ^ 1)))
+    return pairs
 
 
 def gelu_and_slope(v):
@@ -113,6 +154,10 @@
         self.send_sem, self.recv_sem = send_sem, recv_sem
         self.sent = []
         self.used = 0
+        self.notes = []
+
+    def note(self, mark):
+        self.notes.append(mark)
 
     def take(self, count):
         self.used += count
@@ -151,6 +196,9 @@
     def send(self, m, ref, to):
         self.mail.send(self.base + m, ref, ref, self.peers[to])
 
+    def numbers(self, *messages):
+        return [self.base + m for m in messages]
+
     def got(self, m, ref):
         self.mail.arrived(self.base + m, ref, self.peers["sibling"])
 
@@ -163,7 +211,7 @@
         self.send(2, own, "up")
         self.send(3, own, "down")
         self.send(1, own, "sibling")
-        yield
+        yield self.numbers(2, 3)
         for q, first, fwd in ((p, 2, 7), (1 - p, 4, 11)):
             if first == 4:
                 ref = self.region(q, t, k)
@@ -171,7 +219,7 @@
                 self.send(4, ref, "up")
                 self.send(5, ref, "down")
                 self.send(6, ref, "sibling")
-                yield
+                yield self.numbers(4, 5)
             ref = self.region(q, before, k)
             self.got(first, ref)
             self.send(fwd, self.half(q, before, k, 0), "up")
@@ -180,12 +228,12 @@
             self.got(first + 1, ref)
             self.send(fwd + 2, self.half(q, after, k, 1), "down")
             self.send(fwd + 3, ref, "sibling")
-            yield
+            yield self.numbers(0) if first == 2 else self.numbers(7, 9)
         for q, fwd, last in ((p, 7, 15), (1 - p, 11, 16)):
             self.got(fwd, self.half(q, far, k, 0))
             self.got(fwd + 2, self.half(q, far, k, 1))
             self.send(last, self.region(q, far, k), "sibling")
-            yield
+            yield self.numbers(11, 13) if last == 15 else self.numbers(1, 6, 8, 10, 12, 14, 15, 16)
         for m, q, s in (
             (1, p, t),
             (6, 1 - p, t),
@@ -255,13 +303,15 @@
             four = pl.ds(pl.multiple_of(side[q] * 4 * PART, 4 * PART), 4 * PART)
             src = part.at[pl.ds(first_row(n, side[q], 0, 1 - k), 4 * PART)]
             mail.send(sib + q, src, from_sibling.at[four], peers["sibling"])
-        yield
+        yield [sib + 1]
 
         def chip_sum(q, s):
             own = first_row(n, side[q], (t + s) % RING, k)
             add_rows(sums, cell(q, s), part, own, from_sibling, cell(q, s), PART)
 
         for q in (1, 0):
+            if q == 0:
+                yield [sib]
             four = pl.ds(pl.multiple_of(side[q] * 4 * PART, 4 * PART), 4 * PART)
             got(sib + q, from_sibling.at[four])
             chip_sum(q, 2)
@@ -282,8 +332,8 @@
             )
         for q in (1, 0):
             chip_sum(q, 0)
-        yield
         for q in (1, 0):
+            yield [far + 2 * q, far + 2 * q + 1]
             got(far + 2 * q, from_far.at[2 * q])
             c = cell(q, 1)
             add_rows(sums, c, sums, c, from_far.at[2 * q], 0, half)
@@ -302,7 +352,6 @@
                 from_near.at[2 * q + 1, pl.ds(half, half)],
                 peers["down"],
             )
-            yield
 
         def wait_near(q):
             got(nearby + 4 * q, from_near.at[2 * q, pl.ds(half, half)])
@@ -318,6 +367,7 @@
                 + from_near[2 * q + 1, rows].astype(f32)
             )
 
+        yield [nearby + 4 + i for i in range(4)]
         wait_near(1)
 
         def pair_part(i, _):
@@ -326,9 +376,9 @@
 
         lax.fori_loop(0, PART // 16, pair_part, 0)
         mail.send(pair, sums.at[pl.ds(cell(1, 0), PART)], from_pair, peers["pair"])
-        yield
+        yield [nearby + i for i in range(4)]
         wait_near(0)
-        yield
+        yield [pair]
         got(pair, from_pair)
 
         def own_part(i, _):
@@ -371,7 +421,7 @@
 
 
 def whole_step(
-    pieces, cot, up_one, down_one, up_two, down_two,
+    pieces, cot, up_one, down_one, up_two, down_two, cot_other, up_other, down_other,
     grad_up_one, grad_down_one, grad_up_two, grad_down_two,
     wide, other, inputs, normed_one, slope_one, act_one, part_one,
     cots, up_home, down_home, mixed, middle, mine, normed_two, act_two, slope_two, part_two,
@@ -450,17 +500,19 @@
 
         chunks(body)
 
-    swaps = {name: Swap(place, mail) for name in ("cot", "up", "down", "grad_up", "grad_down")}
+    swaps = {name: Swap(place, mail) for name in ("grad_up", "grad_down")}
 
     def chain(g):
         number = mail.take(1)
-        own = pieces[pl.ds(g * ROWS, ROWS)]
-        wide[pl.ds(g * ROWS, ROWS)] = jnp.concatenate([own, own], axis=1)
+        for path in range(PATHS):
+            own = pieces[pl.ds(path * TOKENS + g * PART, PART)]
+            to = g * ROWS + slot(path // 8, path // 2 % RING, path % 2) * PART
+            wide[pl.ds(to, PART)] = jnp.concatenate([own, own], axis=1)
         there = pl.ds(pl.multiple_of(g * ROWS + (1 - k) * half_rows, half_rows), half_rows)
         here = pl.ds(pl.multiple_of(g * ROWS + k * half_rows, half_rows), half_rows)
         landed = other.at[pl.ds(g * half_rows, half_rows)]
         mail.send(number, wide.at[there], landed, peers_c["sibling"])
-        yield
+        yield [number]
         mail.arrived(number, landed, peers_c["sibling"])
         lane = lax.broadcasted_iota(jnp.int32, (half_rows, 128), 1) // 64
 
@@ -491,28 +543,23 @@
             normed_two.at[pl.ds(my_row(g), PART)],
             normed_two.at[pl.ds(swap_row(g), PART)],
         )
-        yield
+        yield [swap.number]
         swap.wait()
         yield from Gather(row, mail, *token_regions(normed_two, g)).steps()
-        if g == 0:
-            swaps["up"].wait()
-            swaps["down"].wait()
+        if -1 - g not in mail.notes:
+            yield [-1 - g]
+        assert -1 - g in mail.notes
         level_two(g)
         scatter = Scatter(row, mail, g, part_two, row_bufs, back_mine.at[g]).steps()
-        next(scatter)
-        yield
-        next(scatter)
+        yield next(scatter)
+        yield next(scatter)
+        awaited = next(scatter)
         level_two_grads(g)
-        yield
-        if g == GROUPS - 1:
-            ready_up_two[...] = sum_up_two[...].astype(b16)
-            ready_down_two[...] = sum_down_two[...].astype(b16)
-            swaps["grad_up"].start(ready_up_two, grad_up_two, grad_up_two)
-            swaps["grad_down"].start(ready_down_two, grad_down_two, grad_down_two)
+        yield awaited
         yield from scatter
         swap = Swap(place, mail)
         swap.start(back_mine.at[g], back.at[g], back.at[g])
-        yield
+        yield [swap.number]
         swap.wait()
         upstream = back[g].astype(f32)
         values = middle[g]
@@ -522,63 +569,52 @@
         )
         own_cot = cot[pl.ds(g * PART, PART)].astype(f32)
         group[pl.ds(first_row(g, col.p, col.t, col.k), PART)] = (own_cot + through).astype(b16)
-        yield from Gather(col, mail, *token_regions(group, g)).steps()
+        for step, awaited in enumerate(Gather(col, mail, *token_regions(group, g)).steps()):
+            if step == LATE and g == GROUPS - 1:
+                ready_up_two[...] = sum_up_two[...].astype(b16)
+                ready_down_two[...] = sum_down_two[...].astype(b16)
+                swaps["grad_up"].start(ready_up_two, grad_up_two, grad_up_two)
+                swaps["grad_down"].start(ready_down_two, grad_down_two, grad_down_two)
+            yield awaited
         level_one_back(g)
+
+    def keep_or_take(dst, own, other):
+        @pl.when(place.stay)
+        def _():
+            dst[...] = own[...]
+
+        @pl.when(jnp.logical_not(place.stay))
+        def _():
+            dst[...] = other[...]
 
     def background():
         for ref in (grad_up_one, grad_down_one, sum_up_two, sum_down_two):
             ref[...] = jnp.zeros_like(ref)
-        cot_swaps = [Swap(place, mail) for _ in range(GROUPS)]
-        for g, swap in enumerate(cot_swaps):
-            swap.start(
+        for g in range(GROUPS):
+            keep_or_take(
+                cots.at[pl.ds(my_row(g), PART)],
                 cot.at[pl.ds(g * PART, PART)],
-                cots.at[pl.ds(my_row(g), PART)],
-                cots.at[pl.ds(swap_row(g), PART)],
+                cot_other.at[pl.ds(g * PART, PART)],
             )
-        yield
-        swaps["up"].start(up_two, up_home, up_home)
-        swaps["down"].start(down_two, down_home, down_home)
-        for g, swap in enumerate(cot_swaps):
-            swap.wait()
-        gathers = [Gather(row, mail, *token_regions(cots, g)).steps() for g in range(GROUPS)]
-        while gathers:
-            gathers = [gather for gather in gathers if next(gather, "done") != "done"]
-            yield
-
-    tasks = [(0, chain(0)), (1, background())] + [(LAG * g, chain(g)) for g in range(1, GROUPS)]
-    tick = 0
-    while tasks:
-        left = []
-        for begin, task in tasks:
-            if tick < begin or next(task, "done") != "done":
-                left.append((begin, task))
-        tasks = left
-        tick += 1
+        keep_or_take(up_home, up_two, up_other)
+        keep_or_take(down_home, down_two, down_other)
+        yield []
+        for g in range(GROUPS):
+            yield from Gather(row, mail, *token_regions(cots, g)).steps()
+            mail.note(-1 - g)
+
+    tasks = [chain(g) for g in range(GROUPS)] + [background()]
+    for task in ORDER:
+        next(tasks[int(task)], None)
     swaps["grad_up"].wait()
     swaps["grad_down"].wait()
     mail.finish()
 
 
-def on_device(
-    token_ids,
-    embedding,
-    up_one,
-    down_one,
-    up_two,
-    down_two,
-    moment_up_one,
-    moment_down_one,
-    moment_up_two,
-    moment_down_two,
-    cotangent,
-):
-    sharers = PATHS
-    width, hidden = up_one.shape[1:]
-    ids = token_ids[0].reshape(2, 4, 2, GROUPS, PART).transpose(3, 2, 0, 1, 4).reshape(-1)
-    count = ids.shape[0]
-    pieces = embedding.at[ids].get(mode="promise_in_bounds")
+def gradients(*args):
     vmem = pl.BlockSpec(memory_space=pltpu.VMEM)
-    args = [pieces, cotangent[0, 0], up_one[0], down_one[0], up_two[0], down_two[0]]
+    width, hidden = args[2].shape
+    count = args[0].shape[0]
     out_shape = [jax.ShapeDtypeStruct((hidden, width), f32)] * 2
     out_shape += [jax.ShapeDtypeStruct((hidden, width), b16)] * 2
     tokens_b16 = pltpu.VMEM((count, width), b16)
@@ -613,9 +649,9 @@
         tokens_b16,
     ]
     scratch += scatter_scratch(width) + scatter_scratch(width)
-    messages = GROUPS * (1 + 17 + 15 + 1 + 17 + 15 + 1 + 17 + 1 + 17) + 5
+    messages = GROUPS * (1 + 17 + 15 + 1 + 17 + 15 + 1 + 17 + 17) + 2
     scratch += [pltpu.SemaphoreType.DMA((messages,)), pltpu.SemaphoreType.DMA((messages,))]
-    grad_up_one, grad_down_one, grad_up_two, grad_down_two = pl.pallas_call(
+    return pl.pallas_call(
         whole_step,
         name="whole_step",
         out_shape=out_shape,
@@ -623,30 +659,36 @@
         out_specs=[vmem] * len(out_shape),
         scratch_shapes=scratch,
         compiler_params=pltpu.CompilerParams(
-            collective_id=0, has_side_effects=True, vmem_limit_bytes=60 * 2**20
+            collective_id=COLLECTIVE, has_side_effects=True, vmem_limit_bytes=60 * 2**20
         ),
     )(*args)
-    new_up_one, new_moment_up_one = outer_update(
-        up_one[0], moment_up_one[0], grad_up_one.T, sharers
-    )
-    new_down_one, new_moment_down_one = outer_update(
-        down_one[0], moment_down_one[0], grad_down_one, sharers
-    )
-    new_up_two, new_moment_up_two = outer_update(
-        up_two[0], moment_up_two[0], grad_up_two.T.astype(f32), sharers
-    )
-    new_down_two, new_moment_down_two = outer_update(
-        down_two[0], moment_down_two[0], grad_down_two.astype(f32), sharers
-    )
-    return (
-        new_up_one,
-        new_down_one,
-        new_up_two,
-        new_down_two,
-        new_moment_up_one,
-        new_moment_down_one,
-        new_moment_up_two,
-        new_moment_down_two,
+
+
+def on_device(
+    token_ids,
+    embedding,
+    up_one,
+    down_one,
+    up_two,
+    down_two,
+    moment_up_one,
+    moment_down_one,
+    moment_up_two,
+    moment_down_two,
+    cotangent,
+):
+    sharers = PATHS
+    ids = token_ids[0].reshape(-1)
+    pieces = embedding.at[ids].get(mode="promise_in_bounds")
+    own = (cotangent[0, 0], up_two[0], down_two[0])
+    pairs = swap_pairs()
+    other = [lax.ppermute(part, ("row", "col"), pairs) for part in own]
+    grads = gradients(pieces, own[0], up_one[0], down_one[0], own[1], own[2], *other)
+    return update(
+        grads,
+        (up_one[0], down_one[0], up_two[0], down_two[0]),
+        (moment_up_one[0], moment_down_one[0], moment_up_two[0], moment_down_two[0]),
+        sharers,
     )
 
 

time: 225 us -> 204 us (0.907)
  Pallas kernels: 190 us -> 167 us
  starting transfers between devices: 0 us -> 12.8 us
  local copies, waits for them, and re-layouts: 28.2 us -> 21.2 us
  other arithmetic: 5.93 us -> 0.71 us
    pallas_call x1 -> x2, Pallas kernels: 190 us -> 167 us  [the longest x1 161 us: gradients(): pl.pallas_call(whole_step, name='whole_step', out_shape=out_shape, in_spe...]
    ppermute x0 -> x3, starting transfers between devices: none -> 12.8 us  [on_device(): other = [lax.ppermute(part, ('row', 'col'), pairs) for part in own]]
    unnamed x23 -> x7, local copies, waits for them, and re-layouts: 15.8 us -> 9.06 us
    broadcast_in_dim x2 -> x0, other arithmetic: 5.91 us -> none  [outer_update(): return (new_parameter.astype(b16)[None], new_moment.astype(b16)[None])]
  transfers between devices with their start and end apart: 0 -> 3, of which waited for: 0 -> 1; matrix products, arithmetic and copies ran while one was open for 0% -> 10% of each run, Pallas kernels for 0% -> 0%
where the time goes in v3:
time: 204 us
  Pallas kernels  167 us (82%)
  local copies, waits for them, and re-layouts  21.2 us (10%)
  starting transfers between devices  12.8 us (6%)
    pallas_call x1, Pallas kernels, gradients(): pl.pallas_call(whole_step, name='whole_step', out_shape=out_shape, in_spe...  161 us
    ppermute x3, starting transfers between devices, on_device(): other = [lax.ppermute(part, ('row', 'col'), pairs) for part in own]  12.8 us
    gather x1, local copies, waits for them, and re-layouts, on_device(): pieces = embedding.at[ids].get(mode='promise_in_bounds')  12.1 us
    unnamed x7, local copies, waits for them, and re-layouts  9.06 us
    pallas_call x1, Pallas kernels, update(): pl.pallas_call(functools.partial(update_kernel, sharers), name='update',...  5.28 us
  transfers between devices with their start and end apart: 3, of which 1 were waited for; matrix products, arithmetic and copies ran while one was open for 10% of the time, Pallas kernels for 0%

profile of v3, /device:TPU:1, one launch (start us, length us, event | category | flops | bytes accessed | tf_op | source)
XLA Modules:
  0.0 203.9 jit_solution(7727171342908375429)
XLA Ops:
  0.6 6.3 %collective-permute-start = (bf16[128,1024]{1,0:T(8,128)(2,1)}, bf16[128,1024]{1,0:T(8,128)(2,1)S(1)}, u32[]{:S(2)}, u32[]{:S(2)}) collective-permute-start(bf16[128,1024]{1,0:T(8,128)(2,1)} %bitcast.25), channel_id=1, source_target_pairs={{1,128},{3,130},{5,132},{7,134},{9,136},{11,138},{13,140},{15,142}... | collective-permute-start | bytes 786440 | tf_op jit(solution)/shard_map/ppermute | solution.py:685
  6.9 1.9 collective-permute-start.1
  8.9 4.5 %collective-permute-start.2 = (bf16[256,1024]{1,0:T(8,128)(2,1)}, bf16[256,1024]{1,0:T(8,128)(2,1)S(1)}, u32[]{:S(2)}, u32[]{:S(2)}) collective-permute-start(bf16[256,1024]{1,0:T(8,128)(2,1)} %bitcast.18), channel_id=1, source_target_pairs={{1,128},{3,130},{5,132},{7,134},{9,136},{11,138},{13,140},{15,142}... | collective-permute-start | bytes 1572872 | tf_op jit(solution)/shard_map/ppermute | solution.py:685
  13.4 0.7 compare_select_fusion
  14.1 8.3 %copy.19 = bf16[32000,64]{1,0:T(8,128)(2,1)} copy(bf16[32000,64]{0,1:T(8,128)(2,1)} %param.12) | data formatting | bytes 8192000 | tf_op args[1]
  22.4 12.1 %gather_fusion = bf16[2048,64]{1,0:T(8,128)(2,1)} fusion(bf16[32000,64]{1,0:T(8,128)(2,1)} %copy.19, s32[2048]{0:T(1024)S(1)} %broadcast_clamp_fusion), kind=kCustom, calls=%fused_computation | custom fusion | bytes 532480 | tf_op jit(solution)/shard_map/gather | solution.py:682
  34.5 0.0 collective-permute-done.cot_other
  34.5 0.0 copy-start.2
  34.5 0.0 collective-permute-done.1.up_other
  34.5 0.0 copy-start
  34.5 2.0 collective-permute-done.2.down_other
  36.5 0.0 copy-start.1
  36.5 0.0 copy-done.2
  36.5 0.0 copy-done
  36.5 0.8 copy-done.1
  37.3 161.2 %whole_step.1 = (f32[256,1024]{1,0:T(8,128)}, f32[256,1024]{1,0:T(8,128)}, bf16[256,1024]{1,0:T(8,128)(2,1)}, bf16[256,1024]{1,0:T(8,128)(2,1)}) custom-call(bf16[2048,64]{1,0:T(8,128)(2,1)} %gather_fusion, bf16[128,1024]{1,0:T(8,128)(2,1)} %bitcast.26, bf16[1024,256]{1,0:T(8,128)(2,1)} %bitcast.11, bf16[256,1024]{1,0:T(8,128)(2,1)} %bitcast.13, ...), custom_call_target="tpu_custom_call" | custom-call | tf_op jit(solution)/shard_map/whole_step/pallas_call | solution.py:654
  198.5 5.3 %update.1 = (bf16[1,1024,256]{2,1,0:T(8,128)(2,1)}, bf16[1,256,1024]{2,1,0:T(8,128)(2,1)}, bf16[1,1024,256]{2,1,0:T(8,128)(2,1)}, bf16[1,256,1024]{2,1,0:T(8,128...) custom-call(f32[256,1024]{1,0:T(8,128)} %get-tuple-element.12.refs_0, ...), custom_call_target="tpu_custom_call" | custom-call | tf_op jit(solution)/shard_map/update/pallas_call | solution.py:54
  (1 shorter events, 0.0 us)
Async XLA Ops:
  0.6 33.9 %collective-permute-start = (bf16[128,1024]{1,0:T(8,128)(2,1)}, bf16[128,1024]{1,0:T(8,128)(2,1)S(1)}, u32[]{:S(2)}, u32[]{:S(2)}) collective-permute-start(bf16[128,1024]{1,0:T(8,128)(2,1)} %bitcast.25), channel_id=1, source_target_pairs={{1,128},{3,130},{5,132},{7,134},{9,136},{11,138},{13,140},{15,142}... | collective-permute-start | bytes 786440 | tf_op jit(solution)/shard_map/ppermute | solution.py:685
  6.9 27.6 %collective-permute-start.1 = (bf16[1024,256]{1,0:T(8,128)(2,1)}, bf16[1024,256]{1,0:T(8,128)(2,1)S(1)}, u32[]{:S(2)}, u32[]{:S(2)}) collective-permute-start(bf16[1024,256]{1,0:T(8,128)(2,1)} %bitcast.15), channel_id=1, source_target_pairs={{1,128},{3,130},{5,132},{7,134},{9,136},{11,138},{13,140},{15,142}... | collective-permute-start | bytes 1572872 | tf_op jit(solution)/shard_map/ppermute | solution.py:685
  8.9 27.6 %collective-permute-start.2 = (bf16[256,1024]{1,0:T(8,128)(2,1)}, bf16[256,1024]{1,0:T(8,128)(2,1)S(1)}, u32[]{:S(2)}, u32[]{:S(2)}) collective-permute-start(bf16[256,1024]{1,0:T(8,128)(2,1)} %bitcast.18), channel_id=1, source_target_pairs={{1,128},{3,130},{5,132},{7,134},{9,136},{11,138},{13,140},{15,142}... | collective-permute-start | bytes 1572872 | tf_op jit(solution)/shard_map/ppermute | solution.py:685
  34.5 2.0 copy-start.2
  34.5 2.0 copy-start
  36.5 0.8 copy-start.1

commit v4 on v3

--- a/solution.py
+++ b/solution.py
@@ -19,13 +19,14 @@
 PART = TOKENS // GROUPS
 ROWS = PATHS * PART
 ORDER = (
-    0, 1, 2, 2, 0, 1, 2, 2, 0, 1, 0, 2, 2, 2, 1, 0, 0, 2, 1, 1, 2, 2, 0, 0, 1, 2, 2, 0, 0, 1,
-    0, 2, 0, 1, 1, 2, 0, 0, 1, 1, 0, 1, 1, 0, 0, 1, 0, 1, 0, 0, 1, 1, 0, 0, 1, 1, 0, 0, 1, 0,
-    1, 0, 0, 1, 1, 0, 1, 0, 1, 1, 0, 1, 1, 0, 0, 1, 0, 0, 1, 0, 1, 0, 1, 1, 1, 1,
+    0, 1, 2, 0, 1, 2, 0, 1, 2, 0, 1, 0, 0, 1, 1, 2, 0, 0, 1, 2, 2, 0, 0, 1, 0, 2, 0, 1, 1, 2,
+    0, 0, 1, 2, 1, 2, 1, 1, 2, 2, 0, 2, 2, 1, 0, 1, 0, 1, 0, 0, 0, 1, 0, 0, 0, 1, 1, 0, 0, 1,
+    0, 1, 0, 0, 1, 1, 0, 1, 1, 0, 1, 1, 0, 0, 1, 0, 1, 0, 0, 1, 1, 0, 0, 1, 1, 1, 1,
 )
 CHUNK = 256
 COLLECTIVE = 0
-LATE = 2
+LATE = 1
+EARLY = 1
 f32, b16 = jnp.float32, jnp.bfloat16
 
 
@@ -46,31 +47,21 @@
 
 def update(grads, weights, moments, sharers):
     hidden, width = weights[1].shape
-    block = hidden // 2
-    up = pl.BlockSpec((width, block), lambda i: (0, i))
-    down = pl.BlockSpec((block, width), lambda i: (i, 0))
-    new_up = pl.BlockSpec((1, width, block), lambda i: (0, 0, i))
-    new_down = pl.BlockSpec((1, block, width), lambda i: (0, i, 0))
+    steps = 4
+    up = pl.BlockSpec((width // steps, hidden), lambda i: (i, 0))
+    up_grad = pl.BlockSpec((hidden, width // steps), lambda i: (0, i))
+    down = pl.BlockSpec((hidden // steps, width), lambda i: (i, 0))
+    new_up = pl.BlockSpec((1, width // steps, hidden), lambda i: (0, i, 0))
+    new_down = pl.BlockSpec((1, hidden // steps, width), lambda i: (0, i, 0))
     return pl.pallas_call(
         functools.partial(update_kernel, sharers),
         name="update",
-        grid=(2,),
+        grid=(steps,),
         out_shape=[jax.ShapeDtypeStruct((1,) + w.shape, b16) for w in weights] * 2,
-        in_specs=[down] * 4 + [up, down, up, down] * 2,
+        in_specs=[up_grad, down] * 2 + [up, down, up, down] * 2,
         out_specs=[new_up, new_down, new_up, new_down] * 2,
         compiler_params=pltpu.CompilerParams(vmem_limit_bytes=60 * 2**20),
     )(*grads, *weights, *moments)
-
-
-def swap_pairs():
-    pairs = []
-    for zl in range(4):
-        for x in range(4):
-            for col in range(16):
-                if zl // 2 != col % 2:
-                    source = (zl * 4 + x) * 16 + col
-                    pairs.append((source, ((zl + 2) % 4 * 4 + x) * 16 + (col ^ 1)))
-    return pairs
 
 
 def gelu_and_slope(v):
@@ -99,8 +90,8 @@
         row, col = lax.axis_index("row"), lax.axis_index("col")
         self.zl, self.x = row // 4, row % 4
         self.zh, self.y, self.k = col // 8, (col // 2) % 4, col % 2
-        self.stay = (self.zl // 2) == self.k
-        other_zl = (self.zl + 2) % 4
+        self.stay = (self.zl % 2) == self.k
+        other_zl = self.zl + 1 - 2 * (self.zl % 2)
         self.swap = (other_zl * 4 + self.x, self.zh * 8 + self.y * 2 + (1 - self.k))
 
 
@@ -116,11 +107,11 @@
 class RowGroup:
     def __init__(self, place):
         self.place = place
-        self.p, self.t, self.k = place.zl % 2, place.x, place.k
-        self.half = place.zl // 2
+        self.p, self.t, self.k = place.zl // 2, place.x, place.k
+        self.side = place.zl % 2
 
     def device(self, p, t, k):
-        return ((self.half * 2 + p) * 4 + t, self.place.zh * 8 + self.place.y * 2 + k)
+        return ((p * 2 + self.side) * 4 + t, self.place.zh * 8 + self.place.y * 2 + k)
 
 
 def slot(p, t, k):
@@ -421,7 +412,7 @@
 
 
 def whole_step(
-    pieces, cot, up_one, down_one, up_two, down_two, cot_other, up_other, down_other,
+    pieces, cot, up_one, down_one, up_two, down_two,
     grad_up_one, grad_down_one, grad_up_two, grad_down_two,
     wide, other, inputs, normed_one, slope_one, act_one, part_one,
     cots, up_home, down_home, mixed, middle, mine, normed_two, act_two, slope_two, part_two,
@@ -500,7 +491,7 @@
 
         chunks(body)
 
-    swaps = {name: Swap(place, mail) for name in ("grad_up", "grad_down")}
+    swaps = {name: Swap(place, mail) for name in ("up", "down", "grad_up", "grad_down")}
 
     def chain(g):
         number = mail.take(1)
@@ -530,7 +521,11 @@
             at = pl.multiple_of(g * ROWS + k * half_rows + h * quarter, quarter)
             return inputs.at[pl.ds(at, quarter), lanes(p, t)]
 
-        yield from Gather(col, mail, region, half).steps()
+        for step, awaited in enumerate(Gather(col, mail, region, half).steps()):
+            if step == EARLY and g == GROUPS - 1:
+                swaps["up"].start(up_two, up_home, up_home)
+                swaps["down"].start(down_two, down_home, down_home)
+            yield awaited
         level_one(g)
         yield from Scatter(col, mail, g, part_one, col_bufs, mixed).steps()
         own_input = inputs[pl.ds(first_row(g, col.p, col.t, col.k), PART)]
@@ -549,6 +544,10 @@
         if -1 - g not in mail.notes:
             yield [-1 - g]
         assert -1 - g in mail.notes
+        if g == 0:
+            yield [swaps["up"].number, swaps["down"].number]
+            swaps["up"].wait()
+            swaps["down"].wait()
         level_two(g)
         scatter = Scatter(row, mail, g, part_two, row_bufs, back_mine.at[g]).steps()
         yield next(scatter)
@@ -578,27 +577,19 @@
             yield awaited
         level_one_back(g)
 
-    def keep_or_take(dst, own, other):
-        @pl.when(place.stay)
-        def _():
-            dst[...] = own[...]
-
-        @pl.when(jnp.logical_not(place.stay))
-        def _():
-            dst[...] = other[...]
-
     def background():
         for ref in (grad_up_one, grad_down_one, sum_up_two, sum_down_two):
             ref[...] = jnp.zeros_like(ref)
-        for g in range(GROUPS):
-            keep_or_take(
+        cot_swaps = [Swap(place, mail) for _ in range(GROUPS)]
+        for g, swap in enumerate(cot_swaps):
+            swap.start(
+                cot.at[pl.ds(g * PART, PART)],
                 cots.at[pl.ds(my_row(g), PART)],
-                cot.at[pl.ds(g * PART, PART)],
-                cot_other.at[pl.ds(g * PART, PART)],
+                cots.at[pl.ds(swap_row(g), PART)],
             )
-        keep_or_take(up_home, up_two, up_other)
-        keep_or_take(down_home, down_two, down_other)
-        yield []
+        yield [swap.number for swap in cot_swaps]
+        for g, swap in enumerate(cot_swaps):
+            swap.wait()
         for g in range(GROUPS):
             yield from Gather(row, mail, *token_regions(cots, g)).steps()
             mail.note(-1 - g)
@@ -649,7 +640,7 @@
         tokens_b16,
     ]
     scratch += scatter_scratch(width) + scatter_scratch(width)
-    messages = GROUPS * (1 + 17 + 15 + 1 + 17 + 15 + 1 + 17 + 17) + 2
+    messages = GROUPS * (1 + 17 + 15 + 1 + 17 + 15 + 1 + 17 + 1 + 17) + 4
     scratch += [pltpu.SemaphoreType.DMA((messages,)), pltpu.SemaphoreType.DMA((messages,))]
     return pl.pallas_call(
         whole_step,
@@ -680,10 +671,9 @@
     sharers = PATHS
     ids = token_ids[0].reshape(-1)
     pieces = embedding.at[ids].get(mode="promise_in_bounds")
-    own = (cotangent[0, 0], up_two[0], down_two[0])
-    pairs = swap_pairs()
-    other = [lax.ppermute(part, ("row", "col"), pairs) for part in own]
-    grads = gradients(pieces, own[0], up_one[0], down_one[0], own[1], own[2], *other)
+    grads = gradients(
+        pieces, cotangent[0, 0], up_one[0], down_one[0], up_two[0], down_two[0]
+    )
     return update(
         grads,
         (up_one[0], down_one[0], up_two[0], down_two[0]),

time: 204 us -> 194 us (0.951); the launches traced: 204 us -> 191 us
  starting transfers between devices: 12.8 us -> 0 us
    ppermute x3 -> x0, starting transfers between devices: 12.8 us -> none  [on_device(): other = [lax.ppermute(part, ('row', 'col'), pairs) for part in own]]
    unnamed x7 -> x1, local copies, waits for them, and re-layouts: 9.06 us -> 8.27 us
  transfers between devices with their start and end apart: 3 -> 0, of which waited for: 1 -> 0; matrix products, arithmetic and copies ran while one was open for 10% -> 0% of each run, Pallas kernels for 0% -> 0%
where the time goes in v4:
time: 194 us; the launch traced here: 191 us
  Pallas kernels  169 us (87%)
  local copies, waits for them, and re-layouts  20.4 us (11%)
    pallas_call x1, Pallas kernels, gradients(): pl.pallas_call(whole_step, name='whole_step', out_shape=out_shape, in_spe...  163 us
    gather x1, local copies, waits for them, and re-layouts, on_device(): pieces = embedding.at[ids].get(mode='promise_in_bounds')  12.1 us
    unnamed x1, local copies, waits for them, and re-layouts  8.27 us
    pallas_call x1, Pallas kernels, update(): pl.pallas_call(functools.partial(update_kernel, sharers), name='update',...  6.01 us

profile of v4, /device:TPU:1, one launch (start us, length us, event | category | flops | bytes accessed | tf_op | source)
XLA Modules:
  0.0 190.8 jit_solution(16449785680236658275)
XLA Ops:
  0.6 0.7 compare_select_fusion
  1.4 8.3 %copy.19 = bf16[32000,64]{1,0:T(8,128)(2,1)} copy(bf16[32000,64]{0,1:T(8,128)(2,1)} %param.12) | data formatting | bytes 8192000 | tf_op args[1]
  9.6 12.1 %gather_fusion = bf16[2048,64]{1,0:T(8,128)(2,1)} fusion(bf16[32000,64]{1,0:T(8,128)(2,1)} %copy.19, s32[2048]{0:T(1024)S(1)} %broadcast_clamp_fusion), kind=kCustom, calls=%fused_computation | custom fusion | bytes 532480 | tf_op jit(solution)/shard_map/gather | solution.py:673
  21.7 163.0 %whole_step.1 = (f32[256,1024]{1,0:T(8,128)}, f32[256,1024]{1,0:T(8,128)}, bf16[256,1024]{1,0:T(8,128)(2,1)}, bf16[256,1024]{1,0:T(8,128)(2,1)}) custom-call(bf16[2048,64]{1,0:T(8,128)(2,1)} %gather_fusion, bf16[128,1024]{1,0:T(8,128)(2,1)} %bitcast.23, bf16[1024,256]{1,0:T(8,128)(2,1)} %bitcast.11, bf16[256,1024]{1,0:T(8,128)(2,1)} %bitcast.13, ...), custom_call_target="tpu_custom_call" | custom-call | tf_op jit(solution)/shard_map/whole_step/pallas_call | solution.py:645
  184.7 6.0 %update.1 = (bf16[1,1024,256]{2,1,0:T(8,128)(2,1)}, bf16[1,256,1024]{2,1,0:T(8,128)(2,1)}, bf16[1,1024,256]{2,1,0:T(8,128)(2,1)}, bf16[1,256,1024]{2,1,0:T(8,128...) custom-call(f32[256,1024]{1,0:T(8,128)} %get-tuple-element.12.refs_0, ...), custom_call_target="tpu_custom_call" | custom-call | tf_op jit(solution)/shard_map/update/pallas_call | solution.py:56
  (1 shorter events, 0.0 us)

commit v5 on v4

--- a/solution.py
+++ b/solution.py
@@ -19,14 +19,14 @@
 PART = TOKENS // GROUPS
 ROWS = PATHS * PART
 ORDER = (
-    0, 1, 2, 0, 1, 2, 0, 1, 2, 0, 1, 0, 0, 1, 1, 2, 0, 0, 1, 2, 2, 0, 0, 1, 0, 2, 0, 1, 1, 2,
-    0, 0, 1, 2, 1, 2, 1, 1, 2, 2, 0, 2, 2, 1, 0, 1, 0, 1, 0, 0, 0, 1, 0, 0, 0, 1, 1, 0, 0, 1,
-    0, 1, 0, 0, 1, 1, 0, 1, 1, 0, 1, 1, 0, 0, 1, 0, 1, 0, 0, 1, 1, 0, 0, 1, 1, 1, 1,
+    0, 1, 0, 1, 2, 0, 0, 1, 0, 0, 1, 2, 0, 0, 1, 1, 2, 2, 0, 0, 1, 1, 0, 0, 2, 2, 1, 0, 1, 2,
+    0, 2, 1, 1, 2, 0, 1, 1, 0, 2, 0, 1, 2, 2, 2, 1, 2, 0, 1, 0, 0, 1, 0, 0, 0, 1, 1, 0, 0, 1,
+    1, 0, 0, 1, 1, 0, 0, 1, 1, 1, 1, 0, 0, 1, 0, 0, 1, 0, 0, 1, 1, 0, 0, 1, 1, 1, 1,
 )
 CHUNK = 256
 COLLECTIVE = 0
-LATE = 1
-EARLY = 1
+LATE = 2
+EARLY = 3
 f32, b16 = jnp.float32, jnp.bfloat16
 
 

time: 194 us -> 187 us (0.964)
  Pallas kernels: 169 us -> 163 us
    pallas_call x1, Pallas kernels: 163 us -> 157 us  [gradients(): pl.pallas_call(whole_step, name='whole_step', out_shape=out_shape, in_spe...]
where the time goes in v5:
time: 187 us; the launch traced here: 185 us
  Pallas kernels  163 us (87%)
  local copies, waits for them, and re-layouts  20.4 us (11%)
    pallas_call x1, Pallas kernels, gradients(): pl.pallas_call(whole_step, name='whole_step', out_shape=out_shape, in_spe...  157 us
    gather x1, local copies, waits for them, and re-layouts, on_device(): pieces = embedding.at[ids].get(mode='promise_in_bounds')  12.1 us
    unnamed x1, local copies, waits for them, and re-layouts  8.27 us
    pallas_call x1, Pallas kernels, update(): pl.pallas_call(functools.partial(update_kernel, sharers), name='update',...  6.01 us

profile of v5, /device:TPU:1, one launch (start us, length us, event | category | flops | bytes accessed | tf_op | source)
XLA Modules:
  0.0 185.3 jit_solution(15424804398260814662)
XLA Ops:
  0.6 0.7 compare_select_fusion
  1.4 8.3 %copy.19 = bf16[32000,64]{1,0:T(8,128)(2,1)} copy(bf16[32000,64]{0,1:T(8,128)(2,1)} %param.12) | data formatting | bytes 8192000 | tf_op args[1]
  9.6 12.1 %gather_fusion = bf16[2048,64]{1,0:T(8,128)(2,1)} fusion(bf16[32000,64]{1,0:T(8,128)(2,1)} %copy.19, s32[2048]{0:T(1024)S(1)} %broadcast_clamp_fusion), kind=kCustom, calls=%fused_computation | custom fusion | bytes 532480 | tf_op jit(solution)/shard_map/gather | solution.py:673
  21.7 157.4 %whole_step.1 = (f32[256,1024]{1,0:T(8,128)}, f32[256,1024]{1,0:T(8,128)}, bf16[256,1024]{1,0:T(8,128)(2,1)}, bf16[256,1024]{1,0:T(8,128)(2,1)}) custom-call(bf16[2048,64]{1,0:T(8,128)(2,1)} %gather_fusion, bf16[128,1024]{1,0:T(8,128)(2,1)} %bitcast.23, bf16[1024,256]{1,0:T(8,128)(2,1)} %bitcast.11, bf16[256,1024]{1,0:T(8,128)(2,1)} %bitcast.13, ...), custom_call_target="tpu_custom_call" | custom-call | tf_op jit(solution)/shard_map/whole_step/pallas_call | solution.py:645
  179.1 6.0 %update.1 = (bf16[1,1024,256]{2,1,0:T(8,128)(2,1)}, bf16[1,256,1024]{2,1,0:T(8,128)(2,1)}, bf16[1,1024,256]{2,1,0:T(8,128)(2,1)}, bf16[1,256,1024]{2,1,0:T(8,128...) custom-call(f32[256,1024]{1,0:T(8,128)} %get-tuple-element.12.refs_0, ...), custom_call_target="tpu_custom_call" | custom-call | tf_op jit(solution)/shard_map/update/pallas_call | solution.py:56
  (1 shorter events, 0.0 us)
